TPU v7x, 256 devices: a whole 4x4x8 slice. The times are simulated.
256 devices in a mesh: dom: 256 (over y, x, z, core).
Axes of the slice: x: 4, y: 4, z: 8, core: 2. Of those that a mesh axis runs over, the one named last changes fastest.
Arguments:
- features: bfloat16 [524288, 128], P('dom'), may hold values from -6 to 6
- w_self: bfloat16 [128, 256], replicated, may hold values from -0.5 to 0.5
- w_neigh: bfloat16 [128, 256], replicated, may hold values from -1.75 to 1.75
- cotangent: bfloat16 [524288, 256], P('dom'), may hold values from -6 to 6
- neighbours: int32 [524288, 10], P('dom'), may hold values from 0 to 3327, as said below
- send_rows: int32 [256, 5, 256], P('dom'), may hold values from 0 to 2047, as said below
- send_count: int32 [256, 5], P('dom'), may hold values from 64 to 256, as said below
Outputs:
- hidden: bfloat16 [524288, 256], P('dom')
- grad_features: float32 [524288, 128], P('dom')
- grad_self: float32 [128, 256], replicated
- grad_neigh: float32 [128, 256], replicated
Inputs may be any that keep to these rules, and one draw needn't show every extreme that they name: `neighbours`: entries below 2048 name the partition's own rows; an entry 2048 + b * 256 + c names slot c of round b from partner p XOR 2^b, and c is below that partner's send_count for round b. `send_rows`: local row numbers, all different within one partition's round. Slots 0 to send_count - 1 of a round are live.
All inputs are finite; a program needn't handle non-finite values.
Results may differ from a plain program's by a relative error of at most 0.0059.
Values may be sent and summed in bfloat16 or wider, within the bound.
A program may use at most 64 MiB of HBM per device.

v0:
```python
import jax
import jax.numpy as jnp
from jax import lax
from jax.sharding import PartitionSpec as P

FAN = 10
ROUNDS = 5


def from_partner(value, axis, stride):
    mask = 2**stride
    pairs = [(source, source ^ mask) for source in range(lax.axis_size(axis))]
    return lax.ppermute(value, axis, pairs)


def silu_slope(pre):
    sig = jax.nn.sigmoid(pre)
    return sig * (1.0 + pre * (1.0 - sig))


def count_block(nb_block, columns, dtype):
    column_ids = jnp.arange(columns, dtype=jnp.int32)[None, :]
    counts = jnp.zeros((nb_block.shape[0], columns), jnp.float32)
    for entry in range(FAN):
        counts = counts + (nb_block[:, entry : entry + 1] == column_ids).astype(jnp.float32)
    return counts.astype(dtype)


def picker(rows_one, alive_one, rows, dtype):
    row_ids = jnp.arange(rows, dtype=jnp.int32)[None, :]
    return ((rows_one[:, None] == row_ids).astype(jnp.float32) * alive_one[:, None]).astype(dtype)


def send_boundary(features, rows_sent, alive):
    rows = features.shape[0]
    arrived = []
    for bit in range(ROUNDS):
        choose = picker(rows_sent[bit], alive[bit], rows, jnp.bfloat16)
        outgoing = jnp.dot(choose, features, preferred_element_type=jnp.float32).astype(
            jnp.bfloat16
        )
        arrived.append(from_partner(outgoing, "dom", bit))
    return arrived


def return_rows(grad_feat, back, rows_one, alive_one):
    choose = picker(rows_one, alive_one, grad_feat.shape[0], jnp.float32)
    contract = (((0,), (0,)), ((), ()))
    return grad_feat + lax.dot_general(
        choose, back, contract, precision=lax.Precision.HIGHEST, preferred_element_type=jnp.float32
    )


def on_device(features, w_self, w_neigh, cotangent, neighbours, send_rows, send_count):
    rows = features.shape[0]
    width = features.shape[1]
    cap = send_rows.shape[2]
    extent = rows + ROUNDS * cap
    block_rows = 512
    nb_blocks = neighbours.reshape(rows // block_rows, block_rows, FAN)
    rows_sent = send_rows[0]
    slot = jnp.arange(cap, dtype=jnp.int32)
    alive = (slot[None, :] < send_count[0][:, None]).astype(jnp.float32)
    arrived = send_boundary(features, rows_sent, alive)
    table = jnp.concatenate([features] + arrived, 0)

    def all_sum_rows(nb_block):
        counts = count_block(nb_block, extent, jnp.bfloat16)
        return jnp.dot(counts, table, preferred_element_type=jnp.float32)

    total = lax.map(all_sum_rows, nb_blocks).reshape(rows, width)
    mean_rows = (total / FAN).astype(jnp.bfloat16)
    pre = jnp.dot(features, w_self, preferred_element_type=jnp.float32) + jnp.dot(
        mean_rows, w_neigh, preferred_element_type=jnp.float32
    )
    hidden = jax.nn.silu(pre).astype(jnp.bfloat16)
    grad_pre = (cotangent.astype(jnp.float32) * silu_slope(pre)).astype(jnp.bfloat16)
    contract = (((0,), (0,)), ((), ()))
    trans = (((1,), (1,)), ((), ()))
    part_self = lax.dot_general(features, grad_pre, contract, preferred_element_type=jnp.float32)
    part_neigh = lax.dot_general(mean_rows, grad_pre, contract, preferred_element_type=jnp.float32)
    grad_mean = lax.dot_general(grad_pre, w_neigh, trans, preferred_element_type=jnp.float32) / FAN
    mean_blocks = grad_mean.reshape(rows // block_rows, block_rows, width)

    def spread_block(carry, pieces):
        nb_block, grad_block = pieces
        counts = count_block(nb_block, extent, jnp.float32)
        added = lax.dot_general(
            counts,
            grad_block,
            contract,
            precision=lax.Precision.HIGHEST,
            preferred_element_type=jnp.float32,
        )
        return (carry + added, None)

    grad_table, unused = lax.scan(
        spread_block, jnp.zeros((extent, width), jnp.float32), (nb_blocks, mean_blocks)
    )
    grad_feat = (
        lax.dot_general(grad_pre, w_self, trans, preferred_element_type=jnp.float32)
        + grad_table[:rows]
    )
    for bit in range(ROUNDS):
        outgoing = grad_table[rows + bit * cap : rows + (bit + 1) * cap]
        back = from_partner(outgoing.astype(jnp.bfloat16), "dom", bit).astype(outgoing.dtype)
        grad_feat = return_rows(grad_feat, back, rows_sent[bit], alive[bit])
    sum_self, sum_neigh = lax.psum((part_self, part_neigh), "dom")
    scale = jnp.float32(rows * lax.axis_size("dom")) ** (-0.5)
    return (hidden, grad_feat, sum_self * scale, sum_neigh * scale)


def solution(mesh):
    placed = (
        P("dom", None),
        P(),
        P(),
        P("dom", None),
        P("dom", None),
        P("dom", None, None),
        P("dom", None),
    )
    return jax.shard_map(
        on_device,
        mesh=mesh,
        in_specs=placed,
        out_specs=(P("dom", None), P("dom", None), P(), P()),
        check_vma=False,
    )
```

profile of v0, /device:TPU:1, one launch (start us, length us, event | category | flops | bytes accessed | tf_op | source)
XLA Modules:
  0.0 447.2 jit_solution(8498504473603967106)
XLA Ops:
  7.2 0.8 fusion.94
  8.1 0.8 fusion.109
  8.9 2.2 convolution_convert_fusion.4
  11.0 3.2 collective-permute-start
  14.3 1.1 convolution_convert_fusion.3
  15.5 1.1 convolution_convert_fusion.2
  16.6 2.9 collective-permute-start.2
  19.5 1.1 convolution_convert_fusion.1
  20.6 4.2 collective-permute-start.3
  24.8 1.1 convolution_convert_fusion
  25.9 1.4 collective-permute-start.4
  27.4 1.8 fusion.110
  29.1 0.8 constant_dynamic-update-slice_fusion.5
  30.1 1.5 constant_dynamic-update-slice_fusion.4
  31.5 1.5 constant_dynamic-update-slice_fusion.3
  33.0 1.5 constant_dynamic-update-slice_fusion.2
  34.5 1.5 constant_dynamic-update-slice_fusion.1
  36.0 1.5 constant_dynamic-update-slice_fusion
  37.5 39.9 %while.21 = (s32[]{:T(128)}, f32[4,512,128]{2,1,0:T(8,128)S(1)}, s32[4,512,10]{1,2,0:T(8,128)S(1)}, bf16[3328,128]{1,0:T(8,128)(2,1)}, s32[]{:T(128)}) while((s32[]{:T(128)}, f32[4,512,128]{2,1,0:T(8,128)S(1)}, s32[4,512,10]{1,2,0:T(8,128)S(1)}, bf16[3328,128]{1,0:T(8,128)(2,1)}, s32[]{:T(128)}) %tuple.80), condition=%wide.region_1.2_spmd, body=%wide.region_0.1_spmd.sunk | while | flops 487325696 | bytes 1216581 | solution.py:71
  37.5 9.9 %fusion.144 = f32[4,512,128]{2,1,0:T(8,128)S(1)} fusion(f32[4,512,128]{2,1,0:T(8,128)S(1)} %get-tuple-element.238, s32[]{:T(128)} %get-tuple-element.237, bf16[3328,128]{1,0:T(8,128)(2,1)} %get-tuple-element.245, s32[512]{0:T(512)S(1)} %bitcast.135, s32[512]{0:T(512)S(1)} %bitcast.136, s32[512]{0:T(512)S(1)} %bitcast.137, s32[512]{0:T(512)S(1)} %bitcast.138, ...), kind=kOutput, calls=%fused_computation.13.clone.1 | convolution fusion | flops 487325696 | bytes 1134596 | tf_op jit(solution)/shard_map/while/body/eval_jaxpr/dot_general | solution.py:69
  47.4 9.9 %fusion.144 = f32[4,512,128]{2,1,0:T(8,128)S(1)} fusion(f32[4,512,128]{2,1,0:T(8,128)S(1)} %get-tuple-element.238, s32[]{:T(128)} %get-tuple-element.237, bf16[3328,128]{1,0:T(8,128)(2,1)} %get-tuple-element.245, s32[512]{0:T(512)S(1)} %bitcast.135, s32[512]{0:T(512)S(1)} %bitcast.136, s32[512]{0:T(512)S(1)} %bitcast.137, s32[512]{0:T(512)S(1)} %bitcast.138, ...), kind=kOutput, calls=%fused_computation.13.clone.1 | convolution fusion | flops 487325696 | bytes 1134596 | tf_op jit(solution)/shard_map/while/body/eval_jaxpr/dot_general | solution.py:69
  57.4 9.9 %fusion.144 = f32[4,512,128]{2,1,0:T(8,128)S(1)} fusion(f32[4,512,128]{2,1,0:T(8,128)S(1)} %get-tuple-element.238, s32[]{:T(128)} %get-tuple-element.237, bf16[3328,128]{1,0:T(8,128)(2,1)} %get-tuple-element.245, s32[512]{0:T(512)S(1)} %bitcast.135, s32[512]{0:T(512)S(1)} %bitcast.136, s32[512]{0:T(512)S(1)} %bitcast.137, s32[512]{0:T(512)S(1)} %bitcast.138, ...), kind=kOutput, calls=%fused_computation.13.clone.1 | convolution fusion | flops 487325696 | bytes 1134596 | tf_op jit(solution)/shard_map/while/body/eval_jaxpr/dot_general | solution.py:69
  67.4 9.9 %fusion.144 = f32[4,512,128]{2,1,0:T(8,128)S(1)} fusion(f32[4,512,128]{2,1,0:T(8,128)S(1)} %get-tuple-element.238, s32[]{:T(128)} %get-tuple-element.237, bf16[3328,128]{1,0:T(8,128)(2,1)} %get-tuple-element.245, s32[512]{0:T(512)S(1)} %bitcast.135, s32[512]{0:T(512)S(1)} %bitcast.136, s32[512]{0:T(512)S(1)} %bitcast.137, s32[512]{0:T(512)S(1)} %bitcast.138, ...), kind=kOutput, calls=%fused_computation.13.clone.1 | convolution fusion | flops 487325696 | bytes 1134596 | tf_op jit(solution)/shard_map/while/body/eval_jaxpr/dot_general | solution.py:69
  77.5 4.1 multiply_convert_fusion
  81.5 1.2 fusion.111
  82.7 1.4 convolution_multiply_fusion
  84.1 95.9 %while.22 = (s32[]{:T(128)}, f32[3328,128]{1,0:T(8,128)S(1)}, s32[4,512,10]{1,2,0:T(8,128)S(1)}, f32[4,512,128]{2,1,0:T(8,128)}, s32[]{:T(128)}, /*index=5*/s32[]{:T(128)}) while((s32[]{:T(128)}, f32[3328,128]{1,0:T(8,128)S(1)}, s32[4,512,10]{1,2,0:T(8,128)S(1)}, f32[4,512,128]{2,1,0:T(8,128)}, s32[]{:T(128)}, ...), condition=%wide.region_3.4_spmd.clone, body=%wide.region_2.3_spmd.clone.sunk | while | flops 2667511808 | bytes 3773011 | solution.py:97
  97.4 0.6 fusion.147
  98.1 19.9 %fusion.148 = f32[3328,128]{1,0:T(8,128)S(1)} fusion(s32[512]{0:T(512)S(1)} %bitcast.125, s32[512]{0:T(512)S(1)} %bitcast.126, s32[512]{0:T(512)S(1)} %bitcast.127, s32[512]{0:T(512)} %bitcast.128, s32[512]{0:T(512)} %bitcast.129, s32[512]{0:T(512)} %bitcast.130, s32[512]{0:T(512)} %bitcast.131, s32[512]{0:T(512)} %bitcast.132, s32[512]{0:T(512)} %bitcast.133, ...), kind=kOutput, calls=%fused_computation.45.clone.1 | convolution fusion | flops 2667511808 | bytes 3691009 | tf_op jit(solution)/shard_map/while/body/eval_jaxpr/dot_general | solution.py:88
  118.7 19.9 %fusion.148 = f32[3328,128]{1,0:T(8,128)S(1)} fusion(s32[512]{0:T(512)S(1)} %bitcast.125, s32[512]{0:T(512)S(1)} %bitcast.126, s32[512]{0:T(512)S(1)} %bitcast.127, s32[512]{0:T(512)} %bitcast.128, s32[512]{0:T(512)} %bitcast.129, s32[512]{0:T(512)} %bitcast.130, s32[512]{0:T(512)} %bitcast.131, s32[512]{0:T(512)} %bitcast.132, s32[512]{0:T(512)} %bitcast.133, ...), kind=kOutput, calls=%fused_computation.45.clone.1 | convolution fusion | flops 2667511808 | bytes 3691009 | tf_op jit(solution)/shard_map/while/body/eval_jaxpr/dot_general | solution.py:88
  139.3 19.9 %fusion.148 = f32[3328,128]{1,0:T(8,128)S(1)} fusion(s32[512]{0:T(512)S(1)} %bitcast.125, s32[512]{0:T(512)S(1)} %bitcast.126, s32[512]{0:T(512)S(1)} %bitcast.127, s32[512]{0:T(512)} %bitcast.128, s32[512]{0:T(512)} %bitcast.129, s32[512]{0:T(512)} %bitcast.130, s32[512]{0:T(512)} %bitcast.131, s32[512]{0:T(512)} %bitcast.132, s32[512]{0:T(512)} %bitcast.133, ...), kind=kOutput, calls=%fused_computation.45.clone.1 | convolution fusion | flops 2667511808 | bytes 3691009 | tf_op jit(solution)/shard_map/while/body/eval_jaxpr/dot_general | solution.py:88
  159.2 0.6 fusion.147
  159.9 19.9 %fusion.148 = f32[3328,128]{1,0:T(8,128)S(1)} fusion(s32[512]{0:T(512)S(1)} %bitcast.125, s32[512]{0:T(512)S(1)} %bitcast.126, s32[512]{0:T(512)S(1)} %bitcast.127, s32[512]{0:T(512)} %bitcast.128, s32[512]{0:T(512)} %bitcast.129, s32[512]{0:T(512)} %bitcast.130, s32[512]{0:T(512)} %bitcast.131, s32[512]{0:T(512)} %bitcast.132, s32[512]{0:T(512)} %bitcast.133, ...), kind=kOutput, calls=%fused_computation.45.clone.1 | convolution fusion | flops 2667511808 | bytes 3691009 | tf_op jit(solution)/shard_map/while/body/eval_jaxpr/dot_general | solution.py:88
  180.0 1.4 convolution_add_fusion.1
  181.6 1.3 collective-permute-start.8
  182.9 1.1 convolution_bitcast_fusion
  184.0 0.7 collective-permute-start.6
  185.2 2.2 collective-permute-start.5
  187.5 2.0 collective-permute-done.8
  189.5 1.9 fusion.41
  191.5 1.9 fusion.43
  193.5 1.9 fusion.45
  195.5 1.9 fusion.39
  197.4 3.0 fusion.61
  200.5 237.0 %all-reduce.3.cloned.1.call-done = (f32[128,256]{0,1:T(8,128)}, f32[128,256]{0,1:T(8,128)}) async-done(((f32[128,256]{0,1:T(8,128)}, f32[128,256]{0,1:T(8,128)}), (f32[128,256]{0,1:T(8,128)}, f32[128,256]{0,1:T(8,128)})) %all-reduce.3.cloned.1.call-update) | async-done | bytes 262160 | tf_op jit(solution)/shard_map/psum | solution.py:108
  437.5 1.0 broadcast_multiply_fusion
  438.5 0.8 copy.20
  439.3 0.8 copy.21
  (88 shorter events, 2.4 us)
Async XLA Ops:
  7.2 70.3 %copy-start = (bf16[128,256]{1,0:T(8,128)(2,1)S(1)}, bf16[128,256]{1,0:T(8,128)(2,1)}, u32[]{:S(2)}) copy-start(bf16[128,256]{1,0:T(8,128)(2,1)} %param.13) | copy-start | bytes 196612
  7.2 7.1 %copy-start.1 = (bf16[2048,128]{1,0:T(8,128)(2,1)S(1)}, bf16[2048,128]{1,0:T(8,128)(2,1)}, u32[]{:S(2)}) copy-start(bf16[2048,128]{1,0:T(8,128)(2,1)} %param.11) | copy-start | bytes 1572868
  7.2 430.3 %all-reduce.3.cloned.1.call-start = ((), (), s32[]{:S(2)}) async-start(), calls=%async_computation | async-start | bytes 524288 | tf_op jit(solution)/shard_map/psum | solution.py:108
  8.0 7.3 %copy-start.6 = (f32[1,256]{1,0:T(1,128)}, f32[1,256]{1,0:T(1,128)S(1)}, u32[]{:S(2)}) copy-start(f32[1,256]{1,0:T(1,128)S(1)} %get-tuple-element.134) | copy-start | bytes 3076
  8.0 7.3 %copy-start.14 = (f32[1,256]{1,0:T(1,128)}, f32[1,256]{1,0:T(1,128)S(1)}, u32[]{:S(2)}) copy-start(f32[1,256]{1,0:T(1,128)S(1)} %get-tuple-element.133) | copy-start | bytes 3076
  8.0 7.4 %copy-start.18 = (f32[1,256]{1,0:T(1,128)}, f32[1,256]{1,0:T(1,128)S(1)}, u32[]{:S(2)}) copy-start(f32[1,256]{1,0:T(1,128)S(1)} %get-tuple-element.132) | copy-start | bytes 3076
  8.1 11.4 %copy-start.22 = (f32[1,256]{1,0:T(1,128)}, f32[1,256]{1,0:T(1,128)S(1)}, u32[]{:S(2)}) copy-start(f32[1,256]{1,0:T(1,128)S(1)} %get-tuple-element.131) | copy-start | bytes 3076
  8.1 16.7 %copy-start.10 = (f32[1,256]{1,0:T(1,128)}, f32[1,256]{1,0:T(1,128)S(1)}, u32[]{:S(2)}) copy-start(f32[1,256]{1,0:T(1,128)S(1)} %get-tuple-element.130) | copy-start | bytes 3076
  8.8 6.6 %copy-start.8 = (s32[1,1,256]{2,0,1:T(1,128)}, s32[1,1,256]{2,0,1:T(1,128)S(1)}, u32[]{:S(2)}) copy-start(s32[1,1,256]{2,0,1:T(1,128)S(1)} %get-tuple-element.138) | copy-start | bytes 3076
  8.8 6.6 %copy-start.16 = (s32[1,1,256]{2,0,1:T(1,128)}, s32[1,1,256]{2,0,1:T(1,128)S(1)}, u32[]{:S(2)}) copy-start(s32[1,1,256]{2,0,1:T(1,128)S(1)} %get-tuple-element.137) | copy-start | bytes 3076
  8.8 6.7 %copy-start.20 = (s32[1,1,256]{2,0,1:T(1,128)}, s32[1,1,256]{2,0,1:T(1,128)S(1)}, u32[]{:S(2)}) copy-start(s32[1,1,256]{2,0,1:T(1,128)S(1)} %get-tuple-element.136) | copy-start | bytes 3076
  8.8 10.7 %copy-start.24 = (s32[1,1,256]{2,0,1:T(1,128)}, s32[1,1,256]{2,0,1:T(1,128)S(1)}, u32[]{:S(2)}) copy-start(s32[1,1,256]{2,0,1:T(1,128)S(1)} %get-tuple-element.139) | copy-start | bytes 3076
  8.8 16.0 %copy-start.12 = (s32[1,1,256]{2,0,1:T(1,128)}, s32[1,1,256]{2,0,1:T(1,128)S(1)}, u32[]{:S(2)}) copy-start(s32[1,1,256]{2,0,1:T(1,128)S(1)} %get-tuple-element.135) | copy-start | bytes 3076
  11.0 19.0 %collective-permute-start = (bf16[256,128]{1,0:T(8,128)(2,1)}, bf16[256,128]{1,0:T(8,128)(2,1)}, u32[]{:S(2)}, u32[]{:S(2)}) collective-permute-start(bf16[256,128]{1,0:T(8,128)(2,1)} %convolution_convert_fusion.4), channel_id=1, source_target_pairs={{0,1},{1,0},{2,3},{3,2},{4,5},{5,4},{6,7},{7,6},{8,9},{9,8},{10,11... | collective-permute-start | bytes 196616 | tf_op jit(solution)/shard_map/ppermute | solution.py:13
  15.4 16.2 %collective-permute-start.1 = (bf16[256,128]{1,0:T(8,128)(2,1)}, bf16[256,128]{1,0:T(8,128)(2,1)}, u32[]{:S(2)}, u32[]{:S(2)}) collective-permute-start(bf16[256,128]{1,0:T(8,128)(2,1)} %convolution_convert_fusion.3), channel_id=1, source_target_pairs={{0,2},{1,3},{2,0},{3,1},{4,6},{5,7},{6,4},{7,5},{8,10},{9,11},{10,... | collective-permute-start | bytes 196616 | tf_op jit(solution)/shard_map/ppermute | solution.py:13
  16.6 16.4 %collective-permute-start.2 = (bf16[256,128]{1,0:T(8,128)(2,1)}, bf16[256,128]{1,0:T(8,128)(2,1)}, u32[]{:S(2)}, u32[]{:S(2)}) collective-permute-start(bf16[256,128]{1,0:T(8,128)(2,1)} %convolution_convert_fusion.2), channel_id=1, source_target_pairs={{0,4},{1,5},{2,6},{3,7},{4,0},{5,1},{6,2},{7,3},{8,12},{9,13},{10,... | collective-permute-start | bytes 196616 | tf_op jit(solution)/shard_map/ppermute | solution.py:13
  19.5 7.9 %copy-start.3 = (bf16[128,256]{1,0:T(8,128)(2,1)S(1)}, bf16[128,256]{1,0:T(8,128)(2,1)}, u32[]{:S(2)}) copy-start(bf16[128,256]{1,0:T(8,128)(2,1)} %param.12) | copy-start | bytes 196612
  20.6 13.9 %collective-permute-start.3 = (bf16[256,128]{1,0:T(8,128)(2,1)}, bf16[256,128]{1,0:T(8,128)(2,1)}, u32[]{:S(2)}, u32[]{:S(2)}) collective-permute-start(bf16[256,128]{1,0:T(8,128)(2,1)} %convolution_convert_fusion.1), channel_id=1, source_target_pairs={{0,8},{1,9},{2,10},{3,11},{4,12},{5,13},{6,14},{7,15},{8,0},{9,1},... | collective-permute-start | bytes 196616 | tf_op jit(solution)/shard_map/ppermute | solution.py:13
  25.9 4.0 copy-start.5
  25.9 10.1 %collective-permute-start.4 = (bf16[256,128]{1,0:T(8,128)(2,1)}, bf16[256,128]{1,0:T(8,128)(2,1)}, u32[]{:S(2)}, u32[]{:S(2)}) collective-permute-start(bf16[256,128]{1,0:T(8,128)(2,1)} %convolution_convert_fusion), channel_id=1, source_target_pairs={{0,16},{1,17},{2,18},{3,19},{4,20},{5,21},{6,22},{7,23},{8,24},{9,... | collective-permute-start | bytes 196616 | tf_op jit(solution)/shard_map/ppermute | solution.py:13
  84.1 95.9 %copy-start.4 = (bf16[128,256]{1,0:T(8,128)(2,1)S(1)}, bf16[128,256]{1,0:T(8,128)(2,1)}, u32[]{:S(2)}) copy-start(bf16[128,256]{1,0:T(8,128)(2,1)} %param.12) | copy-start | bytes 196612
  181.5 8.1 %copy-start.23 = (f32[1,256]{1,0:T(1,128)S(1)}, f32[1,256]{1,0:T(1,128)}, u32[]{:S(2)}) copy-start(f32[1,256]{1,0:T(1,128)} %copy-done.22) | copy-start | bytes 3076
  181.5 8.1 %copy-start.25 = (s32[1,1,256]{2,0,1:T(1,128)S(1)}, s32[1,1,256]{2,0,1:T(1,128)}, u32[]{:S(2)}) copy-start(s32[1,1,256]{2,0,1:T(1,128)} %copy-done.24) | copy-start | bytes 3076
  181.5 9.9 %copy-start.19 = (f32[1,256]{1,0:T(1,128)S(1)}, f32[1,256]{1,0:T(1,128)}, u32[]{:S(2)}) copy-start(f32[1,256]{1,0:T(1,128)} %copy-done.18) | copy-start | bytes 3076
  181.6 9.9 %copy-start.21 = (s32[1,1,256]{2,0,1:T(1,128)S(1)}, s32[1,1,256]{2,0,1:T(1,128)}, u32[]{:S(2)}) copy-start(s32[1,1,256]{2,0,1:T(1,128)} %copy-done.20) | copy-start | bytes 3076
  181.6 7.9 %collective-permute-start.8 = (bf16[256,128]{1,0:T(8,128)(2,1)S(1)}, bf16[256,128]{1,0:T(8,128)(2,1)S(1)}, u32[]{:S(2)}, u32[]{:S(2)}) collective-permute-start(bf16[256,128]{1,0:T(8,128)(2,1)S(1)} %get-tuple-element.127), channel_id=1, source_target_pairs={{0,8},{1,9},{2,10},{3,11},{4,12},{5,13},{6,14},{7,15},{8,0},{9,1},... | collective-permute-start | bytes 196616 | tf_op jit(solution)/shard_map/ppermute | solution.py:13
  184.0 9.5 %copy-start.15 = (f32[1,256]{1,0:T(1,128)S(1)}, f32[1,256]{1,0:T(1,128)}, u32[]{:S(2)}) copy-start(f32[1,256]{1,0:T(1,128)} %copy-done.14) | copy-start | bytes 3076
  184.0 9.5 %copy-start.17 = (s32[1,1,256]{2,0,1:T(1,128)S(1)}, s32[1,1,256]{2,0,1:T(1,128)}, u32[]{:S(2)}) copy-start(s32[1,1,256]{2,0,1:T(1,128)} %copy-done.16) | copy-start | bytes 3076
  184.0 7.5 %collective-permute-start.7 = (bf16[256,128]{1,0:T(8,128)(2,1)S(1)}, bf16[256,128]{1,0:T(8,128)(2,1)S(1)}, u32[]{:S(2)}, u32[]{:S(2)}) collective-permute-start(bf16[256,128]{1,0:T(8,128)(2,1)S(1)} %get-tuple-element.128), channel_id=1, source_target_pairs={{0,4},{1,5},{2,6},{3,7},{4,0},{5,1},{6,2},{7,3},{8,12},{9,13},{10,... | collective-permute-start | bytes 196616 | tf_op jit(solution)/shard_map/ppermute | solution.py:13
  184.0 9.5 %collective-permute-start.6 = (bf16[256,128]{1,0:T(8,128)(2,1)S(1)}, bf16[256,128]{1,0:T(8,128)(2,1)S(1)}, u32[]{:S(2)}, u32[]{:S(2)}) collective-permute-start(bf16[256,128]{1,0:T(8,128)(2,1)S(1)} %get-tuple-element.129), channel_id=1, source_target_pairs={{0,2},{1,3},{2,0},{3,1},{4,6},{5,7},{6,4},{7,5},{8,10},{9,11},{10,... | collective-permute-start | bytes 196616 | tf_op jit(solution)/shard_map/ppermute | solution.py:13
  184.7 10.7 %collective-permute-start.9 = (bf16[256,128]{1,0:T(8,128)(2,1)S(1)}, bf16[256,128]{1,0:T(8,128)(2,1)S(1)}, u32[]{:S(2)}, u32[]{:S(2)}) collective-permute-start(bf16[256,128]{1,0:T(8,128)(2,1)S(1)} %get-tuple-element.126), channel_id=1, source_target_pairs={{0,16},{1,17},{2,18},{3,19},{4,20},{5,21},{6,22},{7,23},{8,24},{9,... | collective-permute-start | bytes 196616 | tf_op jit(solution)/shard_map/ppermute | solution.py:13
  185.2 12.2 %collective-permute-start.5 = (bf16[256,128]{1,0:T(8,128)(2,1)S(1)}, bf16[256,128]{1,0:T(8,128)(2,1)S(1)}, u32[]{:S(2)}, u32[]{:S(2)}) collective-permute-start(bf16[256,128]{1,0:T(8,128)(2,1)S(1)} %get-tuple-element.125), channel_id=1, source_target_pairs={{0,1},{1,0},{2,3},{3,2},{4,5},{5,4},{6,7},{7,6},{8,9},{9,8},{10,11... | collective-permute-start | bytes 196616 | tf_op jit(solution)/shard_map/ppermute | solution.py:13
  191.5 4.0 copy-start.11
  191.5 4.0 copy-start.13
  193.4 4.0 copy-start.2
  193.4 4.0 copy-start.7
  193.5 4.0 copy-start.9
Sparse Core Ops, SparseCore 0:
  187.6 249.8 all-reduce.2
where the time goes:
time: 453 us; the launch traced here: 447 us
  waiting for transfers between devices  239 us (53%)
  matrix products  148 us (33%)
  starting transfers between devices  16.6 us (4%)
  between operations  14.8 us (3%)
  loops' own time  13.6 us (3%)
  local copies, waits for them, and re-layouts  13.3 us (3%)
    psum x1, waiting for transfers between devices, on_device(): sum_self, sum_neigh = lax.psum((part_self, part_neigh), 'dom')  237 us
    dot_general x4, matrix products, spread_block(): lax.dot_general(counts, grad_block, contract, precision=lax.Precision.HIG...  79.8 us
    dot_general x4, matrix products, all_sum_rows(): return jnp.dot(counts, table, preferred_element_type=jnp.float32)  39.8 us
    ppermute x10, starting transfers between devices, from_partner(): return lax.ppermute(value, axis, pairs)  16.6 us
    another operation x1, loops' own time, on_device(): lax.scan(spread_block, jnp.zeros((extent, width), jnp.float32), (nb_block...  13.6 us
    dot_general x5, matrix products, return_rows(): lax.dot_general(choose, back, contract, precision=lax.Precision.HIGHEST,...  10.7 us
  transfers between devices with their start and end apart: 11, of which 2 were waited for; matrix products, arithmetic and copies ran while one was open for 6% of the time, Pallas kernels for 0%

commit v1 on v0

v1 whole, which is shorter than its diff:
```python
import functools

import jax
import jax.numpy as jnp
from jax import lax
from jax.experimental import pallas as pl
from jax.experimental.pallas import tpu as pltpu
from jax.sharding import PartitionSpec as P

FAN = 10
ROUNDS = 5
CAP = 256
ROWS = 2048
EXT = ROWS + ROUNDS * CAP
D = 128
H = 256
GROUP = 32
ZS = 8
WORDS = 8
DIGITS = 7
MESH = pl.DeviceIdType.MESH
f32, bf16, i32 = jnp.float32, jnp.bfloat16, jnp.int32
ORDER = (3, 2, 4, 1, 0)


def partner_of(me, b):
    bit = (me // 2**b) % 2
    return me + (1 - 2 * bit) * 2**b


def build_counts(l, nbt_ref, val_ref, ct_ref):
    nb = nbt_ref[:, pl.ds(l, 128)]
    one = jnp.int32(1) << (4 * (nb >> 9))
    group = (nb >> 6) & 7
    val_ref[0] = nb & 63
    for q in range(WORDS):
        val_ref[1 + q] = jnp.where(group == q, one, 0)
    for half in range(2):
        rid = lax.broadcasted_iota(i32, (32, 128), 0) + 32 * half
        acc = [jnp.zeros((32, 128), i32)] * WORDS
        for k in range(FAN):
            hit = val_ref[0, k : k + 1, :] == rid
            for q in range(WORDS):
                acc[q] = acc[q] + jnp.where(hit, val_ref[1 + q, k : k + 1, :], 0)
        for q in range(WORDS):
            for s in range(DIGITS):
                row = s * 512 + q * 64 + half * 32
                if row < EXT:
                    digit = acc[q] & jnp.int32(15 << (4 * s))
                    ct_ref[row : row + 32, pl.ds(l, 128)] = digit.astype(f32).astype(bf16)


def kernel(
    feat_hbm, ws_ref, wn_ref, cot_hbm, nbt_ref, key_ref,
    hid_hbm, gf_hbm, gws_ref, gwn_ref,
    ct, pt, fv, xt, tt, cotv, gp, hidv, gm, own, hs, hr, bs, br,
    wcat, wt, val, gw, gwc, rsr, zr, agr,
    in_sem, out_sem, hs_s, hs_r, bs_s, bs_r, rs_s, rs_r, z_s, z_r, ag_s, ag_r,
):
    me = lax.axis_index("dom")
    core = me % 2
    z = (me // 2) % ZS
    xy = me // (2 * ZS)
    m = xy * 2 + core

    def member(mm):
        return (mm // 2) * (2 * ZS) + z * 2 + mm % 2

    def at_z(zz):
        return xy * (2 * ZS) + zz * 2 + core

    get_feat = pltpu.make_async_copy(feat_hbm, fv, in_sem.at[0])
    get_cot = pltpu.make_async_copy(cot_hbm, cotv, in_sem.at[1])
    get_feat.start()
    get_cot.start()

    barrier = pltpu.get_barrier_semaphore()

    def greet(j, c):
        pl.semaphore_signal(barrier, inc=1, device_id=(member((m + j) % GROUP),), device_id_type=MESH)
        return c

    lax.fori_loop(1, GROUP, greet, 0)

    def greet_z(j, c):
        pl.semaphore_signal(barrier, inc=1, device_id=(at_z((z + j) % ZS),), device_id_type=MESH)
        return c

    lax.fori_loop(1, ZS, greet_z, 0)

    wcat[0:D, :] = ws_ref[...]
    wcat[D : 2 * D, :] = wn_ref[...]
    wt[:, 0:D] = wn_ref[...].T
    wt[:, D : 2 * D] = ws_ref[...].T
    get_feat.wait()
    for s in range(4):
        piece = fv[512 * s : 512 * (s + 1), :].T
        xt[0:D, 512 * s : 512 * (s + 1)] = piece
        tt[:, 512 * s : 512 * (s + 1)] = piece * jnp.bfloat16(16.0**-s)

    def halo(b):
        return pltpu.make_async_remote_copy(
            src_ref=hs.at[b], dst_ref=hr.at[b], send_sem=hs_s.at[b], recv_sem=hs_r.at[b],
            device_id=(partner_of(me, b),), device_id_type=MESH)

    for at, b in enumerate(ORDER):
        def pick(i, c, b=b):
            r = pl.multiple_of(i * 256, 256)
            ids = lax.broadcasted_iota(i32, (256, CAP), 0) + r
            hit = key_ref[b : b + 1, :] == ids
            pt[pl.ds(r, 256), b * CAP : (b + 1) * CAP] = jnp.where(hit, 1.0, 0.0).astype(bf16)
            return c

        lax.fori_loop(0, ROWS // 256, pick, 0)
        hs[b] = jnp.dot(
            xt[0:D, :], pt[:, b * CAP : (b + 1) * CAP], preferred_element_type=f32).astype(bf16)
        if at == 0:
            pl.semaphore_wait(barrier, GROUP - 1 + ZS - 1)
        halo(b).start()

    def build(i, c):
        build_counts(pl.multiple_of(i * 128, 128), nbt_ref, val, ct)
        return c

    lax.fori_loop(0, ROWS // 128, build, 0)

    for b in ORDER:
        halo(b).wait()
        s = (ROWS + b * CAP) // 512
        tt[:, ROWS + b * CAP : ROWS + (b + 1) * CAP] = hr[b] * jnp.bfloat16(16.0**-s)

    get_cot.wait()
    NB = 512

    def put_hid(i):
        return pltpu.make_async_copy(
            hidv.at[pl.ds(i * NB, NB)], hid_hbm.at[pl.ds(i * NB, NB)], out_sem.at[i])

    def dense(i, c):
        l = pl.multiple_of(i * NB, NB)
        total = jnp.dot(tt[...], ct[:, pl.ds(l, NB)], preferred_element_type=f32)
        mean_t = (total * (1.0 / FAN)).astype(bf16)
        xt[D : 2 * D, pl.ds(l, NB)] = mean_t
        x = jnp.concatenate([fv[pl.ds(l, NB), :], mean_t.T], axis=1)
        pre = jnp.dot(x, wcat[...], preferred_element_type=f32)
        sig = 1.0 / (1.0 + jnp.exp(-pre))
        hidv[pl.ds(l, NB), :] = (pre * sig).astype(bf16)
        slope = sig * (1.0 + pre * (1.0 - sig))
        grad = (cotv[pl.ds(l, NB), :].astype(f32) * slope).astype(bf16)
        gp[pl.ds(l, NB), :] = grad
        both = jnp.dot(grad, wt[...], preferred_element_type=f32)
        gm[pl.ds(l, NB), :] = (both[:, 0:D] * (1.0 / FAN)).astype(bf16)
        own[pl.ds(l, NB), :] = both[:, D : 2 * D]
        return c

    lax.fori_loop(0, ROWS // NB, dense, 0)
    for i in range(ROWS // NB):
        put_hid(i).start()

    gw[...] = jnp.dot(xt[...], gp[...], preferred_element_type=f32)
    for c in range(GROUP):
        gwc[c] = jnp.concatenate([gw[8 * c : 8 * c + 8, 0:D], gw[8 * c : 8 * c + 8, D:H]], axis=0).astype(bf16)

    def rs(j):
        to = (m + j) % GROUP
        return pltpu.make_async_remote_copy(
            src_ref=gwc.at[to], dst_ref=rsr.at[j], send_sem=rs_s.at[j], recv_sem=rs_r.at[j],
            device_id=(member(to),), device_id_type=MESH)

    def rs_start(j, c):
        rs(j).start()
        return c

    lax.fori_loop(1, GROUP, rs_start, 0)

    def back(b):
        return pltpu.make_async_remote_copy(
            src_ref=bs.at[b], dst_ref=br.at[pl.ds(b * CAP, CAP)], send_sem=bs_s.at[b], recv_sem=bs_r.at[b],
            device_id=(partner_of(me, b),), device_id_type=MESH)

    for b in ORDER:
        row = ROWS + b * CAP
        g = jnp.dot(ct[row : row + CAP, :], gm[...], preferred_element_type=f32)
        bs[b] = (g * (16.0 ** -(row // 512))).astype(bf16)
        back(b).start()

    rsr[0] = gwc[m]

    def rs_wait(j, c):
        rs(j).wait()
        return c

    lax.fori_loop(1, GROUP, rs_wait, 0)
    part = rsr[0].astype(f32)
    for j in range(1, GROUP):
        part = part + rsr[j].astype(f32)
    zr[z] = part

    def zx(j):
        return pltpu.make_async_remote_copy(
            src_ref=zr.at[z], dst_ref=zr.at[z], send_sem=z_s.at[j], recv_sem=z_r.at[j],
            device_id=(at_z((z + j) % ZS),), device_id_type=MESH)

    def z_start(j, c):
        zx(j).start()
        return c

    lax.fori_loop(1, ZS, z_start, 0)

    def local_back(s):
        g = jnp.dot(ct[512 * s : 512 * (s + 1), :], gm[...], preferred_element_type=f32)
        own[512 * s : 512 * (s + 1), :] += g * (16.0**-s)

    local_back(0)
    local_back(1)

    def z_wait(j, c):
        zx(j).wait_send()
        frm = (z + ZS - j) % ZS
        pltpu.make_async_remote_copy(
            src_ref=zr.at[z], dst_ref=zr.at[frm], send_sem=z_s.at[j], recv_sem=z_r.at[j],
            device_id=(at_z(frm),), device_id_type=MESH).wait_recv()
        return c

    lax.fori_loop(1, ZS, z_wait, 0)
    full = zr[0]
    for j in range(1, ZS):
        full = full + zr[j]
    agr[m] = (full * (2.0**-9.5)).astype(bf16)

    def ag(j):
        return pltpu.make_async_remote_copy(
            src_ref=agr.at[m], dst_ref=agr.at[m], send_sem=ag_s.at[j], recv_sem=ag_r.at[j],
            device_id=(member((m + j) % GROUP),), device_id_type=MESH)

    def ag_start(j, c):
        ag(j).start()
        return c

    lax.fori_loop(1, GROUP, ag_start, 0)
    local_back(2)
    local_back(3)

    for b in ORDER:
        back(b).wait()

    def put_gf(i):
        return pltpu.make_async_copy(
            own.at[pl.ds(i * NB, NB)], gf_hbm.at[pl.ds(i * NB, NB)], out_sem.at[4 + i])

    for i in range(ROWS // NB):
        own[NB * i : NB * (i + 1), :] += jnp.dot(
            pt[NB * i : NB * (i + 1), :], br[...], preferred_element_type=f32)
        put_gf(i).start()

    def ag_wait(j, c):
        ag(j).wait_send()
        frm = (m + GROUP - j) % GROUP
        pltpu.make_async_remote_copy(
            src_ref=agr.at[m], dst_ref=agr.at[frm], send_sem=ag_s.at[j], recv_sem=ag_r.at[j],
            device_id=(member(frm),), device_id_type=MESH).wait_recv()
        return c

    lax.fori_loop(1, GROUP, ag_wait, 0)
    for c in range(GROUP):
        chunk = agr[c].astype(f32)
        ref = gws_ref if c < 16 else gwn_ref
        r = 8 * (c % 16)
        ref[r : r + 8, 0:D] = chunk[0:8]
        ref[r : r + 8, D:H] = chunk[8:16]
    for i in range(ROWS // NB):
        put_hid(i).wait()
        put_gf(i).wait()


def on_device(features, w_self, w_neigh, cotangent, neighbours, send_rows, send_count):
    slot = jnp.arange(CAP, dtype=i32)
    key = jnp.where(slot[None, :] < send_count[0][:, None], send_rows[0], -1)
    vmem = pl.BlockSpec(memory_space=pltpu.VMEM)
    hbm = pl.BlockSpec(memory_space=pl.ANY)
    dma = pltpu.SemaphoreType.DMA
    call = pl.pallas_call(
        kernel,
        out_shape=(
            jax.ShapeDtypeStruct((ROWS, H), bf16),
            jax.ShapeDtypeStruct((ROWS, D), f32),
            jax.ShapeDtypeStruct((D, H), f32),
            jax.ShapeDtypeStruct((D, H), f32),
        ),
        in_specs=[hbm, vmem, vmem, hbm, vmem, vmem],
        out_specs=(hbm, hbm, vmem, vmem),
        scratch_shapes=[
            pltpu.VMEM((EXT, ROWS), bf16),
            pltpu.VMEM((ROWS, ROUNDS * CAP), bf16),
            pltpu.VMEM((ROWS, D), bf16),
            pltpu.VMEM((2 * D, ROWS), bf16),
            pltpu.VMEM((D, EXT), bf16),
            pltpu.VMEM((ROWS, H), bf16),
            pltpu.VMEM((ROWS, H), bf16),
            pltpu.VMEM((ROWS, H), bf16),
            pltpu.VMEM((ROWS, D), bf16),
            pltpu.VMEM((ROWS, D), f32),
            pltpu.VMEM((ROUNDS, D, CAP), bf16),
            pltpu.VMEM((ROUNDS, D, CAP), bf16),
            pltpu.VMEM((ROUNDS, CAP, D), bf16),
            pltpu.VMEM((ROUNDS * CAP, D), bf16),
            pltpu.VMEM((2 * D, H), bf16),
            pltpu.VMEM((H, 2 * D), bf16),
            pltpu.VMEM((1 + WORDS, FAN, 128), i32),
            pltpu.VMEM((2 * D, H), f32),
            pltpu.VMEM((GROUP, 16, D), bf16),
            pltpu.VMEM((GROUP, 16, D), bf16),
            pltpu.VMEM((ZS, 16, D), f32),
            pltpu.VMEM((GROUP, 16, D), bf16),
            dma((2,)), dma((8,)),
            dma((ROUNDS,)), dma((ROUNDS,)), dma((ROUNDS,)), dma((ROUNDS,)),
            dma((GROUP,)), dma((GROUP,)), dma((ZS,)), dma((ZS,)), dma((GROUP,)), dma((GROUP,)),
        ],
        compiler_params=pltpu.CompilerParams(
            collective_id=0, has_side_effects=True, vmem_limit_bytes=48 * 1024 * 1024),
        cost_estimate=pl.CostEstimate(flops=4_500_000_000, bytes_accessed=6_000_000, transcendentals=1_000_000),
    )
    return call(features, w_self, w_neigh, cotangent, neighbours.T, key)


def solution(mesh):
    placed = (
        P("dom", None), P(), P(), P("dom", None), P("dom", None), P("dom", None, None), P("dom", None),
    )
    return jax.shard_map(
        on_device,
        mesh=mesh,
        in_specs=placed,
        out_specs=(P("dom", None), P("dom", None), P(), P()),
        check_vma=False,
    )
```

time: 453 us -> 55 us (0.12); the launches traced: 447 us -> 54.7 us
  waiting for transfers between devices: 239 us -> 0 us
  matrix products: 148 us -> 0 us
  Pallas kernels: 0 us -> 44.5 us
  starting transfers between devices: 16.6 us -> 0 us
  between operations: 14.8 us -> 0.65 us
  loops' own time: 13.6 us -> 0 us
  local copies, waits for them, and re-layouts: 13.3 us -> 8.75 us
    psum x1 -> x0, waiting for transfers between devices: 237 us -> none  [on_device(): sum_self, sum_neigh = lax.psum((part_self, part_neigh), 'dom')]
    dot_general x24 -> x0, matrix products: 148 us -> none  [the longest x4 79.8 us: spread_block(): lax.dot_general(counts, grad_block, contract, precision=lax.Precision.HIG...]
    pallas_call x0 -> x1, Pallas kernels: none -> 44.5 us  [on_device(): return call(features, w_self, w_neigh, cotangent, neighbours.T, key)]
    ppermute x10 -> x0, starting transfers between devices: 16.6 us -> none  [from_partner(): return lax.ppermute(value, axis, pairs)]
    another operation x2 -> x0, loops' own time: 13.6 us -> none  [the longest x1 13.6 us: on_device(): lax.scan(spread_block, jnp.zeros((extent, width), jnp.float32), (nb_block...]
  transfers between devices with their start and end apart: 11 -> 0, of which waited for: 2 -> 0; matrix products, arithmetic and copies ran while one was open for 6% -> 0% of each run, Pallas kernels for 0% -> 0%
where the time goes in v1:
time: 55 us; the launch traced here: 54.7 us
  Pallas kernels  44.5 us (81%)
  local copies, waits for them, and re-layouts  8.75 us (16%)
  other arithmetic  0.76 us (1%)
  between operations  0.65 us (1%)
    pallas_call x1, Pallas kernels, on_device(): return call(features, w_self, w_neigh, cotangent, neighbours.T, key)  44.5 us
    unnamed x16, local copies, waits for them, and re-layouts  8.75 us

profile of v1, /device:TPU:1, one launch (start us, length us, event | category | flops | bytes accessed | tf_op | source)
XLA Modules:
  0.0 54.7 jit_solution(6464825656814111194)
XLA Ops:
  0.6 0.0 copy-start.5
  0.6 0.6 %copy-done.5 = s32[1,5]{1,0:T(1,128)S(1)} copy-done((s32[1,5]{1,0:T(1,128)S(1)}, s32[1,5]{1,0:T(1,128)}, u32[]{:S(2)}) %copy-start.5) | copy-done | bytes 44
  1.3 0.8 %bitcast_select_fusion.key_ref = s32[5,256]{1,0:T(8,128)S(1)} fusion(s32[1,5,256]{2,0,1:T(1,128)} %param.12, s32[5]{0:T(128)S(1)} %bitcast.5), kind=kLoop, calls=%fused_computation | loop fusion | flops 2560 | bytes 10260 | tf_op jit(solution)/shard_map/jit(_where)/select_n | solution.py:278
  2.0 0.0 copy-start
  2.0 1.2 %copy-done = bf16[2048,256]{1,0:T(8,128)(2,1)S(1)} copy-done((bf16[2048,256]{1,0:T(8,128)(2,1)S(1)}, bf16[2048,256]{1,0:T(8,128)(2,1)}, u32[]{:S(2)}) %copy-start) | copy-done | bytes 1048600
  3.3 0.0 copy-start.1
  3.3 1.0 %copy-done.1 = bf16[2048,128]{1,0:T(8,128)(2,1)S(1)} copy-done((bf16[2048,128]{1,0:T(8,128)(2,1)S(1)}, bf16[2048,128]{1,0:T(8,128)(2,1)}, u32[]{:S(2)}) %copy-start.1) | copy-done | bytes 524312
  4.3 0.0 copy-start.2
  4.3 0.9 %copy-done.2 = s32[2048,10]{0,1:T(8,128)S(1)} copy-done((s32[2048,10]{0,1:T(8,128)S(1)}, s32[2048,10]{0,1:T(8,128)}, u32[]{:S(2)}) %copy-start.2) | copy-done | bytes 81944
  5.2 0.0 copy-start.3
  5.2 0.8 %copy-done.3 = bf16[128,256]{1,0:T(8,128)(2,1)S(1)} copy-done((bf16[128,256]{1,0:T(8,128)(2,1)S(1)}, bf16[128,256]{1,0:T(8,128)(2,1)}, u32[]{:S(2)}) %copy-start.3) | copy-done | bytes 65560
  6.1 0.0 copy-start.4
  6.1 0.8 %copy-done.4 = bf16[128,256]{1,0:T(8,128)(2,1)S(1)} copy-done((bf16[128,256]{1,0:T(8,128)(2,1)S(1)}, bf16[128,256]{1,0:T(8,128)(2,1)}, u32[]{:S(2)}) %copy-start.4) | copy-done | bytes 65560
  6.9 44.5 %shard_map.102 = (bf16[2048,256]{1,0:T(8,128)(2,1)S(1)}, f32[2048,128]{1,0:T(8,128)S(1)}, f32[128,256]{1,0:T(8,128)S(1)}, f32[128,256]{1,0:T(8,128)S(1)}) custom-call(bf16[2048,128]{1,0:T(8,128)(2,1)S(1)} %copy-done.1, bf16[128,256]{1,0:T(8,128)(2,1)S(1)} %copy-done.3, bf16[128,256]{1,0:T(8,128)(2,1)S(1)} %copy-done.4, bf16[2048,256]{1,0:T(8,128)(2,1)S(1)} %copy-done, ...), custom_call_target="tpu_custom_call" | custom-call | flops 4499999744 | bytes 6000000 | tf_op jit(solution)/shard_map/pallas_call | solution.py:323
  51.4 1.0 %copy.17 = bf16[2048,256]{1,0:T(8,128)(2,1)} copy(bf16[2048,256]{1,0:T(8,128)(2,1)S(1)} %get-tuple-element.8) | data formatting | bytes 2097152
  52.4 1.0 %copy.18 = f32[2048,128]{1,0:T(8,128)} copy(f32[2048,128]{1,0:T(8,128)S(1)} %get-tuple-element.9) | data formatting | bytes 2097152
  53.4 0.7 %copy.19 = f32[128,256]{1,0:T(8,128)} copy(f32[128,256]{1,0:T(8,128)S(1)} %get-tuple-element.10) | data formatting | bytes 262144
  54.0 0.7 %copy.20 = f32[128,256]{1,0:T(8,128)} copy(f32[128,256]{1,0:T(8,128)S(1)} %get-tuple-element.11) | data formatting | bytes 262144
Async XLA Ops:
  0.6 0.7 %copy-start.5 = (s32[1,5]{1,0:T(1,128)S(1)}, s32[1,5]{1,0:T(1,128)}, u32[]{:S(2)}) copy-start(s32[1,5]{1,0:T(1,128)} %param.13) | copy-start | bytes 64
  2.0 1.2 %copy-start = (bf16[2048,256]{1,0:T(8,128)(2,1)S(1)}, bf16[2048,256]{1,0:T(8,128)(2,1)}, u32[]{:S(2)}) copy-start(bf16[2048,256]{1,0:T(8,128)(2,1)} %cot_hbm.1) | copy-start | bytes 3145732
  3.3 1.0 %copy-start.1 = (bf16[2048,128]{1,0:T(8,128)(2,1)S(1)}, bf16[2048,128]{1,0:T(8,128)(2,1)}, u32[]{:S(2)}) copy-start(bf16[2048,128]{1,0:T(8,128)(2,1)} %feat_hbm.1) | copy-start | bytes 1572868
  4.3 0.9 %copy-start.2 = (s32[2048,10]{0,1:T(8,128)S(1)}, s32[2048,10]{0,1:T(8,128)}, u32[]{:S(2)}) copy-start(s32[2048,10]{0,1:T(8,128)} %param.11) | copy-start | bytes 245764
  5.2 0.8 %copy-start.3 = (bf16[128,256]{1,0:T(8,128)(2,1)S(1)}, bf16[128,256]{1,0:T(8,128)(2,1)}, u32[]{:S(2)}) copy-start(bf16[128,256]{1,0:T(8,128)(2,1)} %ws_ref.1) | copy-start | bytes 196612
  6.1 0.8 %copy-start.4 = (bf16[128,256]{1,0:T(8,128)(2,1)S(1)}, bf16[128,256]{1,0:T(8,128)(2,1)}, u32[]{:S(2)}) copy-start(bf16[128,256]{1,0:T(8,128)(2,1)} %wn_ref.1) | copy-start | bytes 196612

commit v2 on v1

v2 whole, which is shorter than its diff:
```python
import functools

import jax
import jax.numpy as jnp
from jax import lax
from jax.experimental import pallas as pl
from jax.experimental.pallas import tpu as pltpu
from jax.sharding import PartitionSpec as P

FAN = 10
ROUNDS = 5
CAP = 256
ROWS = 2048
HALF = ROWS // 2
EXT = ROWS + ROUNDS * CAP
D = 128
H = 256
GROUP = 32
ZS = 8
WORDS = 8
DIGITS = 7
MESH = pl.DeviceIdType.MESH
f32, bf16, i32 = jnp.float32, jnp.bfloat16, jnp.int32
ORDER = (3, 2, 4, 1, 0)
STEPS = sorted(
    ((dy, dx, dc) for dy in range(4) for dx in range(4) for dc in range(2)),
    key=lambda step: (step == (0, 0, 0), min(step[0], 4 - step[0]) + min(step[1], 4 - step[1])),
    reverse=True,
)


def partner_of(me, b):
    bit = (me // 2**b) % 2
    return me + (1 - 2 * bit) * 2**b


def build_counts(l, to, nbt_ref, val_ref, ct_ref):
    nb = nbt_ref[:, pl.ds(l, 128)]
    one = jnp.int32(1) << (4 * (nb >> 9))
    group = (nb >> 6) & 7
    val_ref[0] = nb & 63
    for q in range(WORDS):
        val_ref[1 + q] = jnp.where(group == q, one, 0)
    for half in range(2):
        rid = lax.broadcasted_iota(i32, (32, 128), 0) + 32 * half
        acc = [jnp.zeros((32, 128), i32)] * WORDS
        for k in range(FAN):
            hit = val_ref[0, k : k + 1, :] == rid
            for q in range(WORDS):
                acc[q] = acc[q] + jnp.where(hit, val_ref[1 + q, k : k + 1, :], 0)
        for q in range(WORDS):
            for s in range(DIGITS):
                row = s * 512 + q * 64 + half * 32
                if row < EXT:
                    digit = acc[q] & jnp.int32(15 << (4 * s))
                    ct_ref[row : row + 32, pl.ds(to, 128)] = digit.astype(f32).astype(bf16)


def kernel(
    feat_hbm, ws_hbm, wn_hbm, cot_hbm, nbt_hbm, rows_hbm, live_hbm,
    hidv, own, gws_ref, gwn_ref,
    ws_ref, wn_ref, nbt_ref, rows_ref, live_ref, stl, cta, ctb, pt, fv, xt, tt, cotv, gp, gm, hs, hr, bs, br,
    wcat, wt, val, valb, gw, gwc, rsr, zr, agr,
    in_sem, hs_s, hs_r, bs_s, bs_r, rs_s, rs_r, z_s, z_r, ag_s, ag_r,
):
    me = lax.axis_index("dom")
    core = me % 2
    z = (me // 2) % ZS
    xy = me // (2 * ZS)
    m = xy * 2 + core

    def member(mm):
        return (mm // 2) * (2 * ZS) + z * 2 + mm % 2

    def plane(step):
        dy, dx, dc = step
        return ((xy // 4 + dy) % 4) * 8 + ((xy % 4 + dx) % 4) * 2 + (core + dc) % 2

    def at_z(zz):
        return xy * (2 * ZS) + zz * 2 + core

    fetch = [
        pltpu.make_async_copy(src, dst, in_sem.at[i])
        for i, (src, dst) in enumerate((
            (rows_hbm, rows_ref), (live_hbm, live_ref), (feat_hbm, fv), (nbt_hbm, nbt_ref),
            (ws_hbm, ws_ref), (wn_hbm, wn_ref), (cot_hbm, cotv)))
    ]
    for one in fetch:
        one.start()

    barrier = pltpu.get_barrier_semaphore()

    def greet(j, c):
        pl.semaphore_signal(barrier, inc=1, device_id=(member((m + j) % GROUP),), device_id_type=MESH)
        return c

    lax.fori_loop(1, GROUP, greet, 0)

    def greet_z(j, c):
        pl.semaphore_signal(barrier, inc=1, device_id=(at_z((z + j) % ZS),), device_id_type=MESH)
        return c

    lax.fori_loop(1, ZS, greet_z, 0)

    fetch[0].wait()
    fetch[1].wait()
    fetch[2].wait()
    for s in range(4):
        piece = fv[512 * s : 512 * (s + 1), :].T
        xt[0:D, 512 * s : 512 * (s + 1)] = piece
        tt[:, 512 * s : 512 * (s + 1)] = piece * jnp.bfloat16(16.0**-s)

    def halo(b):
        return pltpu.make_async_remote_copy(
            src_ref=hs.at[b], dst_ref=hr.at[b], send_sem=hs_s.at[b], recv_sem=hs_r.at[b],
            device_id=(partner_of(me, b),), device_id_type=MESH)

    for at, b in enumerate(ORDER):
        slot = lax.broadcasted_iota(i32, (1, CAP), 1)
        key = jnp.where(slot < live_ref[0:1, b : b + 1], rows_ref[b], -1)

        def pick(i, c, b=b, key=key):
            r = pl.multiple_of(i * 256, 256)
            ids = lax.broadcasted_iota(i32, (256, CAP), 0) + r
            hit = key == ids
            pt[pl.ds(r, 256), b * CAP : (b + 1) * CAP] = jnp.where(hit, 1.0, 0.0).astype(bf16)
            return c

        lax.fori_loop(0, ROWS // 256, pick, 0)
        hs[b] = jnp.dot(
            xt[0:D, :], pt[:, b * CAP : (b + 1) * CAP], preferred_element_type=f32).astype(bf16)
        if at == 0:
            pl.semaphore_wait(barrier, GROUP - 1 + ZS - 1)
        halo(b).start()

    fetch[3].wait()

    def build_a(i):
        build_counts(pl.multiple_of(i * 128, 128), pl.multiple_of(i * 128, 128), nbt_ref, val, cta)

    def build_b(i):
        build_counts(pl.multiple_of(HALF + i * 128, 128), pl.multiple_of(i * 128, 128), nbt_ref, valb, ctb)

    def sum_own(i, base, ref):
        l = pl.multiple_of(i * 128, 128)
        stl[:, pl.ds(pl.multiple_of(base + i * 128, 128), 128)] = jnp.dot(
            tt[:, 0:ROWS], ref[0:ROWS, pl.ds(l, 128)], preferred_element_type=f32)

    build_a(0)

    def build(i, c):
        sum_own(i, 0, cta)
        build_b(i)
        sum_own(i, HALF, ctb)
        build_a(i + 1)
        return c

    lax.fori_loop(0, HALF // 128 - 1, build, 0)
    sum_own(HALF // 128 - 1, 0, cta)
    build_b(HALF // 128 - 1)
    sum_own(HALF // 128 - 1, HALF, ctb)

    for i in (4, 5, 6):
        fetch[i].wait()
    wcat[0:D, :] = ws_ref[...]
    wcat[D : 2 * D, :] = wn_ref[...]
    wt[:, 0:D] = wn_ref[...].T
    wt[:, D : 2 * D] = ws_ref[...].T

    for b in ORDER:
        halo(b).wait()
        s = (ROWS + b * CAP) // 512
        tt[:, ROWS + b * CAP : ROWS + (b + 1) * CAP] = hr[b] * jnp.bfloat16(16.0**-s)

    NB = 512
    for i in range(ROWS // NB):
        l = i * NB
        ref = cta if l < HALF else ctb
        total = stl[:, l : l + NB] + jnp.dot(
            tt[:, ROWS:EXT], ref[ROWS:EXT, l % HALF : l % HALF + NB], preferred_element_type=f32)
        mean_t = (total * (1.0 / FAN)).astype(bf16)
        xt[D : 2 * D, l : l + NB] = mean_t
        x = jnp.concatenate([fv[l : l + NB, :], mean_t.T], axis=1)
        pre = jnp.dot(x, wcat[...], preferred_element_type=f32)
        sig = 0.5 + 0.5 * jnp.tanh(0.5 * pre)
        hidv[l : l + NB, :] = (pre * sig).astype(bf16)
        slope = sig * (1.0 + pre * (1.0 - sig))
        grad = (cotv[l : l + NB, :].astype(f32) * slope).astype(bf16)
        gp[l : l + NB, :] = grad
        both = jnp.dot(grad, wt[...], preferred_element_type=f32)
        gm[l : l + NB, :] = (both[:, 0:D] * (1.0 / FAN)).astype(bf16)
        own[l : l + NB, :] = both[:, D : 2 * D]

    gw[...] = jnp.dot(xt[...], gp[...], preferred_element_type=f32)
    for c in range(GROUP):
        gwc[c] = jnp.concatenate([gw[8 * c : 8 * c + 8, 0:D], gw[8 * c : 8 * c + 8, D:H]], axis=0).astype(bf16)

    def rs(j):
        to = plane(STEPS[j])
        return pltpu.make_async_remote_copy(
            src_ref=gwc.at[to], dst_ref=rsr.at[j], send_sem=rs_s.at[j], recv_sem=rs_r.at[j],
            device_id=(member(to),), device_id_type=MESH)

    for j in range(1, GROUP):
        rs(j).start()

    def spread(row, count):
        return jnp.dot(
            cta[row : row + count, :], gm[0:HALF, :], preferred_element_type=f32
        ) + jnp.dot(ctb[row : row + count, :], gm[HALF:ROWS, :], preferred_element_type=f32)

    def back(b):
        return pltpu.make_async_remote_copy(
            src_ref=bs.at[b], dst_ref=br.at[pl.ds(b * CAP, CAP)], send_sem=bs_s.at[b], recv_sem=bs_r.at[b],
            device_id=(partner_of(me, b),), device_id_type=MESH)

    for b in ORDER:
        row = ROWS + b * CAP
        g = spread(row, CAP)
        bs[b] = (g * (16.0 ** -(row // 512))).astype(bf16)
        back(b).start()

    rsr[0] = gwc[m]

    for j in range(1, GROUP):
        rs(j).wait()
    part = rsr[0].astype(f32)
    for j in range(1, GROUP):
        part = part + rsr[j].astype(f32)
    zr[z] = part

    def zx(j):
        return pltpu.make_async_remote_copy(
            src_ref=zr.at[z], dst_ref=zr.at[z], send_sem=z_s.at[j], recv_sem=z_r.at[j],
            device_id=(at_z((z + j) % ZS),), device_id_type=MESH)

    for j in (4, 3, 5, 2, 6, 1, 7):
        zx(j).start()

    def local_back(s):
        g = spread(512 * s, 512)
        own[512 * s : 512 * (s + 1), :] += g * (16.0**-s)

    local_back(0)
    local_back(1)

    def z_wait(j):
        zx(j).wait_send()
        frm = (z + ZS - j) % ZS
        pltpu.make_async_remote_copy(
            src_ref=zr.at[z], dst_ref=zr.at[frm], send_sem=z_s.at[j], recv_sem=z_r.at[j],
            device_id=(at_z(frm),), device_id_type=MESH).wait_recv()

    for j in range(1, ZS):
        z_wait(j)
    full = zr[0]
    for j in range(1, ZS):
        full = full + zr[j]
    agr[m] = (full * (2.0**-9.5)).astype(bf16)

    def ag(j):
        return pltpu.make_async_remote_copy(
            src_ref=agr.at[m], dst_ref=agr.at[m], send_sem=ag_s.at[j], recv_sem=ag_r.at[j],
            device_id=(member(plane(STEPS[j])),), device_id_type=MESH)

    for j in range(1, GROUP):
        ag(j).start()
    local_back(2)
    local_back(3)

    for b in ORDER:
        back(b).wait()

    for i in range(ROWS // NB):
        own[NB * i : NB * (i + 1), :] += jnp.dot(
            pt[NB * i : NB * (i + 1), :], br[...], preferred_element_type=f32)

    def ag_wait(j):
        ag(j).wait_send()
        dy, dx, dc = STEPS[j]
        frm = plane((4 - dy, 4 - dx, 2 - dc))
        pltpu.make_async_remote_copy(
            src_ref=agr.at[m], dst_ref=agr.at[frm], send_sem=ag_s.at[j], recv_sem=ag_r.at[j],
            device_id=(member(frm),), device_id_type=MESH).wait_recv()

    for j in range(1, GROUP):
        ag_wait(j)
    for c in range(GROUP):
        chunk = agr[c].astype(f32)
        ref = gws_ref if c < 16 else gwn_ref
        r = 8 * (c % 16)
        ref[r : r + 8, 0:D] = chunk[0:8]
        ref[r : r + 8, D:H] = chunk[8:16]


def hand_over(hid, gf, gws, gwn, hid_out, gf_out, gws_out, gwn_out, sem):
    copies = [
        pltpu.make_async_copy(src, dst, sem.at[i])
        for i, (src, dst) in enumerate(((hid, hid_out), (gf, gf_out), (gws, gws_out), (gwn, gwn_out)))
    ]
    for one in copies:
        one.start()
    for one in copies:
        one.wait()


def on_device(features, w_self, w_neigh, cotangent, neighbours, send_rows, send_count):
    vmem = pl.BlockSpec(memory_space=pltpu.VMEM)
    hbm = pl.BlockSpec(memory_space=pl.ANY)
    dma = pltpu.SemaphoreType.DMA
    shapes = (((ROWS, H), bf16), ((ROWS, D), f32), ((D, H), f32), ((D, H), f32))
    call = pl.pallas_call(
        kernel,
        out_shape=tuple(pltpu.VMEM(*one) for one in shapes),
        in_specs=[hbm] * 7,
        out_specs=(vmem,) * 4,
        scratch_shapes=[
            pltpu.VMEM((D, H), bf16),
            pltpu.VMEM((D, H), bf16),
            pltpu.VMEM((FAN, ROWS), i32),
            pltpu.VMEM((ROUNDS, 1, CAP), i32),
            pltpu.VMEM((1, ROUNDS), i32),
            pltpu.VMEM((D, ROWS), f32),
            pltpu.VMEM((EXT, HALF), bf16),
            pltpu.VMEM((EXT, HALF), bf16),
            pltpu.VMEM((ROWS, ROUNDS * CAP), bf16),
            pltpu.VMEM((ROWS, D), bf16),
            pltpu.VMEM((2 * D, ROWS), bf16),
            pltpu.VMEM((D, EXT), bf16),
            pltpu.VMEM((ROWS, H), bf16),
            pltpu.VMEM((ROWS, H), bf16),
            pltpu.VMEM((ROWS, D), bf16),
            pltpu.VMEM((ROUNDS, D, CAP), bf16),
            pltpu.VMEM((ROUNDS, D, CAP), bf16),
            pltpu.VMEM((ROUNDS, CAP, D), bf16),
            pltpu.VMEM((ROUNDS * CAP, D), bf16),
            pltpu.VMEM((2 * D, H), bf16),
            pltpu.VMEM((H, 2 * D), bf16),
            pltpu.VMEM((1 + WORDS, FAN, 128), i32),
            pltpu.VMEM((1 + WORDS, FAN, 128), i32),
            pltpu.VMEM((2 * D, H), f32),
            pltpu.VMEM((GROUP, 16, D), bf16),
            pltpu.VMEM((GROUP, 16, D), bf16),
            pltpu.VMEM((ZS, 16, D), f32),
            pltpu.VMEM((GROUP, 16, D), bf16),
            dma((7,)),
            dma((ROUNDS,)), dma((ROUNDS,)), dma((ROUNDS,)), dma((ROUNDS,)),
            dma((GROUP,)), dma((GROUP,)), dma((ZS,)), dma((ZS,)), dma((GROUP,)), dma((GROUP,)),
        ],
        compiler_params=pltpu.CompilerParams(
            collective_id=0, has_side_effects=True, vmem_limit_bytes=48 * 1024 * 1024),
        cost_estimate=pl.CostEstimate(flops=4_500_000_000, bytes_accessed=6_000_000, transcendentals=1_000_000),
    )
    args = (features, w_self, w_neigh, cotangent, neighbours.T, send_rows.reshape(ROUNDS, 1, CAP), send_count)
    args = tuple(pltpu.with_memory_space_constraint(one, pltpu.HBM) for one in args)
    return pl.pallas_call(
        hand_over,
        out_shape=tuple(pltpu.HBM(*one) for one in shapes),
        in_specs=[vmem] * 4,
        out_specs=(hbm,) * 4,
        scratch_shapes=[dma((4,))],
    )(*[pltpu.with_memory_space_constraint(one, pltpu.VMEM) for one in call(*args)])


def solution(mesh):
    placed = (
        P("dom", None), P(), P(), P("dom", None), P("dom", None), P("dom", None, None), P("dom", None),
    )
    return jax.shard_map(
        on_device,
        mesh=mesh,
        in_specs=placed,
        out_specs=(P("dom", None), P("dom", None), P(), P()),
        check_vma=False,
    )
```

time: 55 us -> 48.3 us (0.88)
  local copies, waits for them, and re-layouts: 8.75 us -> 0 us
  Pallas kernels: 44.5 us -> 47.4 us
  other arithmetic: 0.76 us -> 0 us
    unnamed x16 -> x0, local copies, waits for them, and re-layouts: 8.75 us -> none
    pallas_call x1 -> x2, Pallas kernels: 44.5 us -> 47.4 us  [the longest x1 46 us: on_device(): call(*args)]
    select_n x1 -> x0, other arithmetic: 0.76 us -> none  [on_device(): key = jnp.where(slot[None, :] < send_count[0][:, None], send_rows[0], -1)]
where the time goes in v2:
time: 48.3 us; the launch traced here: 48.2 us
  Pallas kernels  47.4 us (98%)
  between operations  0.8 us (2%)
    pallas_call x1, Pallas kernels, on_device(): call(*args)  46 us
    pallas_call x1, Pallas kernels, on_device(): pl.pallas_call(hand_over, out_shape=tuple((pltpu.HBM(*one) for one in sha...  1.43 us

profile of v2, /device:TPU:1, one launch (start us, length us, event | category | flops | bytes accessed | tf_op | source)
XLA Modules:
  0.0 48.2 jit_solution(9914779216586667344)
XLA Ops:
  0.6 46.0 %shard_map.102 = (bf16[2048,256]{1,0:T(8,128)(2,1)S(1)}, f32[2048,128]{1,0:T(8,128)S(1)}, f32[128,256]{1,0:T(8,128)S(1)}, f32[128,256]{1,0:T(8,128)S(1)}) custom-call(bf16[2048,128]{1,0:T(8,128)(2,1)} %feat_hbm.1, bf16[128,256]{1,0:T(8,128)(2,1)} %ws_hbm.1, bf16[128,256]{1,0:T(8,128)(2,1)} %wn_hbm.1, bf16[2048,256]{1,0:T(8,128)(2,1)} %cot_hbm.1, ...), custom_call_target="tpu_custom_call" | custom-call | flops 4499999744 | bytes 6000000 | tf_op jit(solution)/shard_map/pallas_call | solution.py:362
  46.7 1.4 %shard_map.103 = (bf16[2048,256]{1,0:T(8,128)(2,1)}, f32[2048,128]{1,0:T(8,128)}, f32[128,256]{1,0:T(8,128)}, f32[128,256]{1,0:T(8,128)}) custom-call(bf16[2048,256]{1,0:T(8,128)(2,1)S(1)} %get-tuple-element.8.hid, f32[2048,128]{1,0:T(8,128)S(1)} %get-tuple-element.9.gf, f32[128,256]{1,0:T(8,128)S(1)} %get-tuple-element.10.gws, ...), custom_call_target="tpu_custom_call" | custom-call | tf_op jit(solution)/shard_map/pallas_call | solution.py:356

commit v3 on v2

v3 whole, which is shorter than its diff:
```python
import functools

import jax
import jax.numpy as jnp
from jax import lax
from jax.experimental import pallas as pl
from jax.experimental.pallas import tpu as pltpu
from jax.sharding import PartitionSpec as P

FAN = 10
ROUNDS = 5
CAP = 256
ROWS = 2048
EXT = ROWS + ROUNDS * CAP
D = 128
H = 256
GROUP = 32
ZS = 8
WORDS = 8
DIGITS = 7
MESH = pl.DeviceIdType.MESH
f32, bf16, i32 = jnp.float32, jnp.bfloat16, jnp.int32
ORDER = (3, 2, 1, 4, 0)


def ring(step, size):
    return min(step, size - step)


PLANE = sorted(
    ((dy, dx, dc) for dy in range(4) for dx in range(4) for dc in range(2)),
    key=lambda t: (t != (0, 0, 0), ring(t[0], 4) + ring(t[1], 4)), reverse=True)
LINE = sorted(range(8), key=lambda t: (t != 0, ring(t, 8)), reverse=True)


def partner_of(me, b):
    bit = (me // 2**b) % 2
    return me + (1 - 2 * bit) * 2**b


def build_counts(l, nbt_ref, val_ref, ct_ref):
    nb = nbt_ref[:, pl.ds(l, 128)]
    one = jnp.int32(1) << (4 * (nb >> 9))
    group = (nb >> 6) & 7
    val_ref[0] = nb & 63
    for q in range(WORDS):
        val_ref[1 + q] = jnp.where(group == q, one, 0)
    for half in range(2):
        rid = lax.broadcasted_iota(i32, (32, 128), 0) + 32 * half
        acc = [jnp.zeros((32, 128), i32)] * WORDS
        for k in range(FAN):
            hit = val_ref[0, k : k + 1, :] == rid
            for q in range(WORDS):
                acc[q] = acc[q] + jnp.where(hit, val_ref[1 + q, k : k + 1, :], 0)
        for q in range(WORDS):
            for s in range(DIGITS):
                row = s * 512 + q * 64 + half * 32
                if row < EXT:
                    digit = acc[q] & jnp.int32(15 << (4 * s))
                    ct_ref[row : row + 32, pl.ds(l, 128)] = digit.astype(f32).astype(bf16)


def kernel(
    feat_hbm, ws_hbm, wn_hbm, cot_hbm, nbt_hbm, rows_hbm, live_hbm,
    hidv, own, gws_ref, gwn_ref,
    ws_ref, wn_ref, nbt_ref, rows_ref, live_ref, stl, ct, pt, fv, xt, tt, cotv, gp, gm, hs, hr, bs, br,
    wcat, wt, val, gw, gwc, rsr, zr, agr, rows_s, ff, picked,
    in_sem, hs_s, hs_r, bs_s, bs_r, rs_s, rs_r, z_s, z_r, ag_s, ag_r,
):
    me = lax.axis_index("dom")
    core = me % 2
    z = (me // 2) % 8
    x = (me // 16) % 4
    y = me // 64
    spot = (y * 4 + x) * 2 + core

    def plane(step, sign=1):
        there = ((y + sign * step[0] + 4) % 4) * 4 + (x + sign * step[1] + 4) % 4
        return there * 2 + (core + step[2]) % 2

    def line(step, sign=1):
        return (z + sign * step + ZS) % ZS

    def at_plane(place):
        return (place // 2) * 16 + z * 2 + place % 2

    def at_line(place):
        return (spot // 2) * 16 + place * 2 + core

    fetch = [
        pltpu.make_async_copy(src, dst, in_sem.at[i])
        for i, (src, dst) in enumerate((
            (rows_hbm, rows_ref), (live_hbm, live_ref), (feat_hbm, fv), (nbt_hbm, nbt_ref),
            (ws_hbm, ws_ref), (wn_hbm, wn_ref), (cot_hbm, cotv), (rows_hbm, rows_s)))
    ]
    for one in fetch:
        one.start()

    barrier = pltpu.get_barrier_semaphore()

    for j in range(GROUP - 1):
        pl.semaphore_signal(barrier, inc=1, device_id=(at_plane(plane(PLANE[j])),), device_id_type=MESH)
    for j in range(ZS - 1):
        pl.semaphore_signal(barrier, inc=1, device_id=(at_line(line(LINE[j])),), device_id_type=MESH)

    def halo(b):
        return pltpu.make_async_remote_copy(
            src_ref=hs.at[b], dst_ref=hr.at[b], send_sem=hs_s.at[b], recv_sem=hs_r.at[b],
            device_id=(partner_of(me, b),), device_id_type=MESH)

    fetch[2].wait()
    ff[...] = fv[...].astype(f32)
    for i in (0, 1, 7):
        fetch[i].wait()
    for at, b in enumerate(ORDER):
        def load(i, c, b=b):
            r = pl.multiple_of(i * 32, 32)
            for t in range(32):
                picked[pl.ds(r + t, 1), :] = ff[pl.ds(rows_s[b, 0, r + t], 1), :]
            return c

        lax.fori_loop(0, CAP // 32, load, 0)
        live = lax.broadcasted_iota(i32, (CAP, D), 0) < live_ref[0:1, b : b + 1]
        hs[b] = jnp.where(live, picked[...], 0.0).astype(bf16)
        if at == 0:
            pl.semaphore_wait(barrier, GROUP + ZS - 2)
        halo(b).start()

    for s in range(4):
        piece = fv[512 * s : 512 * (s + 1), :].T
        xt[0:D, 512 * s : 512 * (s + 1)] = piece
        tt[:, 512 * s : 512 * (s + 1)] = piece * jnp.bfloat16(16.0**-s)

    def owners(b):
        slot = lax.broadcasted_iota(i32, (1, CAP), 1)
        key = jnp.where(slot < live_ref[0:1, b : b + 1], rows_ref[b], -1)

        def pick(i, c):
            r = pl.multiple_of(i * 512, 512)
            hit = key == lax.broadcasted_iota(i32, (512, CAP), 0) + r
            pt[pl.ds(r, 512), b * CAP : (b + 1) * CAP] = jnp.where(hit, 1.0, 0.0).astype(bf16)
            return c

        lax.fori_loop(0, ROWS // 512, pick, 0)

    fetch[3].wait()

    def build(i, c):
        build_counts(pl.multiple_of(i * 128, 128), nbt_ref, val, ct)
        return c

    lax.fori_loop(0, ROWS // 128, build, 0)
    stl[...] = jnp.dot(tt[:, 0:ROWS], ct[0:ROWS, :], preferred_element_type=f32)

    for i in (4, 5, 6):
        fetch[i].wait()
    wcat[0:D, :] = ws_ref[...]
    wcat[D : 2 * D, :] = wn_ref[...]
    wt[:, 0:D] = wn_ref[...].T
    wt[:, D : 2 * D] = ws_ref[...].T

    for b in ORDER:
        halo(b).wait()
        s = (ROWS + b * CAP) // 512
        tt[:, ROWS + b * CAP : ROWS + (b + 1) * CAP] = hr[b].T * jnp.bfloat16(16.0**-s)

    total = stl[...] + jnp.dot(tt[:, ROWS:EXT], ct[ROWS:EXT, :], preferred_element_type=f32)
    xt[D : 2 * D, :] = (total * (1.0 / FAN)).astype(bf16)
    NB = 512

    def pre_of(i):
        l = i * NB
        both_in = jnp.concatenate([fv[l : l + NB, :], xt[D : 2 * D, l : l + NB].T], axis=1)
        return jnp.dot(both_in, wcat[...], preferred_element_type=f32)

    pre = pre_of(0)
    for i in range(ROWS // NB):
        l = i * NB
        later = pre_of(i + 1) if i + 1 < ROWS // NB else None
        sig = 0.5 + 0.5 * jnp.tanh(0.5 * pre)
        silu = pre * sig
        hidv[l : l + NB, :] = silu.astype(bf16)
        slope = sig + silu * (1.0 - sig)
        grad = (cotv[l : l + NB, :].astype(f32) * slope).astype(bf16)
        gp[l : l + NB, :] = grad
        both = jnp.dot(grad, wt[...], preferred_element_type=f32)
        gm[l : l + NB, :] = (both[:, 0:D] * (1.0 / FAN)).astype(bf16)
        own[l : l + NB, :] = both[:, D : 2 * D]
        pre = later

    gw[...] = jnp.dot(xt[...], gp[...], preferred_element_type=f32)
    for c in range(GROUP):
        r = 8 * c
        gwc[c] = jnp.concatenate([gw[r : r + 8, 0:D], gw[r : r + 8, D:H]], axis=0).astype(bf16)

    def rs(j):
        to = plane(PLANE[j])
        return pltpu.make_async_remote_copy(
            src_ref=gwc.at[to], dst_ref=rsr.at[j], send_sem=rs_s.at[j], recv_sem=rs_r.at[j],
            device_id=(at_plane(to),), device_id_type=MESH)

    for j in range(GROUP - 1):
        rs(j).start()

    def spread(row, count):
        return jnp.dot(ct[row : row + count, :], gm[...], preferred_element_type=f32)

    def back(b):
        return pltpu.make_async_remote_copy(
            src_ref=bs.at[b], dst_ref=br.at[pl.ds(b * CAP, CAP)], send_sem=bs_s.at[b], recv_sem=bs_r.at[b],
            device_id=(partner_of(me, b),), device_id_type=MESH)

    for b in ORDER:
        row = ROWS + b * CAP
        g = spread(row, CAP)
        bs[b] = (g * (16.0 ** -(row // 512))).astype(bf16)
        back(b).start()

    def local_back(s):
        own[512 * s : 512 * (s + 1), :] += spread(512 * s, 512) * (16.0**-s)

    local_back(0)
    for b in (0, 1, 2):
        owners(b)
    for j in range(GROUP - 1):
        rs(j).wait()
    part = gwc[spot].astype(f32)
    for j in range(GROUP - 1):
        part = part + rsr[j].astype(f32)
    zr[z] = part.astype(bf16)

    def zx(j):
        return pltpu.make_async_remote_copy(
            src_ref=zr.at[z], dst_ref=zr.at[z], send_sem=z_s.at[j], recv_sem=z_r.at[j],
            device_id=(at_line(line(LINE[j])),), device_id_type=MESH)

    for j in range(ZS - 1):
        zx(j).start()
    for s in (1, 2, 3):
        local_back(s)
    for b in (3, 4):
        owners(b)

    def z_wait(j):
        zx(j).wait_send()
        frm = line(LINE[j], -1)
        pltpu.make_async_remote_copy(
            src_ref=zr.at[z], dst_ref=zr.at[frm], send_sem=z_s.at[j], recv_sem=z_r.at[j],
            device_id=(at_line(frm),), device_id_type=MESH).wait_recv()

    for j in range(ZS - 1):
        z_wait(j)
    full = zr[0].astype(f32)
    for j in range(1, ZS):
        full = full + zr[j].astype(f32)
    agr[spot] = (full * (2.0**-9.5)).astype(bf16)

    def ag(j):
        return pltpu.make_async_remote_copy(
            src_ref=agr.at[spot], dst_ref=agr.at[spot], send_sem=ag_s.at[j], recv_sem=ag_r.at[j],
            device_id=(at_plane(plane(PLANE[j])),), device_id_type=MESH)

    for j in range(GROUP - 1):
        ag(j).start()

    for b in ORDER:
        back(b).wait()

    for i in range(ROWS // NB):
        own[NB * i : NB * (i + 1), :] += jnp.dot(
            pt[NB * i : NB * (i + 1), :], br[...], preferred_element_type=f32)

    def ag_wait(j):
        ag(j).wait_send()
        frm = plane(PLANE[j], -1)
        pltpu.make_async_remote_copy(
            src_ref=agr.at[spot], dst_ref=agr.at[frm], send_sem=ag_s.at[j], recv_sem=ag_r.at[j],
            device_id=(at_plane(frm),), device_id_type=MESH).wait_recv()

    for j in range(GROUP - 1):
        ag_wait(j)
    for c in range(GROUP):
        chunk = agr[c].astype(f32)
        ref = gws_ref if c < GROUP // 2 else gwn_ref
        r = 8 * (c % (GROUP // 2))
        ref[r : r + 8, 0:D] = chunk[0:8]
        ref[r : r + 8, D:H] = chunk[8:16]


def hand_over(hid, gf, gws, gwn, hid_out, gf_out, gws_out, gwn_out, sem):
    copies = [
        pltpu.make_async_copy(src, dst, sem.at[i])
        for i, (src, dst) in enumerate(((hid, hid_out), (gf, gf_out), (gws, gws_out), (gwn, gwn_out)))
    ]
    for one in copies:
        one.start()
    for one in copies:
        one.wait()


def on_device(features, w_self, w_neigh, cotangent, neighbours, send_rows, send_count):
    vmem = pl.BlockSpec(memory_space=pltpu.VMEM)
    hbm = pl.BlockSpec(memory_space=pl.ANY)
    dma = pltpu.SemaphoreType.DMA
    shapes = (((ROWS, H), bf16), ((ROWS, D), f32), ((D, H), f32), ((D, H), f32))
    call = pl.pallas_call(
        kernel,
        out_shape=tuple(pltpu.VMEM(*one) for one in shapes),
        in_specs=[hbm] * 7,
        out_specs=(vmem,) * 4,
        scratch_shapes=[
            pltpu.VMEM((D, H), bf16),
            pltpu.VMEM((D, H), bf16),
            pltpu.VMEM((FAN, ROWS), i32),
            pltpu.VMEM((ROUNDS, 1, CAP), i32),
            pltpu.VMEM((1, ROUNDS), i32),
            pltpu.VMEM((D, ROWS), f32),
            pltpu.VMEM((EXT, ROWS), bf16),
            pltpu.VMEM((ROWS, ROUNDS * CAP), bf16),
            pltpu.VMEM((ROWS, D), bf16),
            pltpu.VMEM((2 * D, ROWS), bf16),
            pltpu.VMEM((D, EXT), bf16),
            pltpu.VMEM((ROWS, H), bf16),
            pltpu.VMEM((ROWS, H), bf16),
            pltpu.VMEM((ROWS, D), bf16),
            pltpu.VMEM((ROUNDS, CAP, D), bf16),
            pltpu.VMEM((ROUNDS, CAP, D), bf16),
            pltpu.VMEM((ROUNDS, CAP, D), bf16),
            pltpu.VMEM((ROUNDS * CAP, D), bf16),
            pltpu.VMEM((2 * D, H), bf16),
            pltpu.VMEM((H, 2 * D), bf16),
            pltpu.VMEM((1 + WORDS, FAN, 128), i32),
            pltpu.VMEM((2 * D, H), f32),
            pltpu.VMEM((GROUP, 16, D), bf16),
            pltpu.VMEM((GROUP, 16, D), bf16),
            pltpu.VMEM((ZS, 16, D), bf16),
            pltpu.VMEM((GROUP, 16, D), bf16),
            pltpu.SMEM((ROUNDS, 1, CAP), i32),
            pltpu.VMEM((ROWS, D), f32),
            pltpu.VMEM((CAP, D), f32),
            dma((8,)),
            dma((ROUNDS,)), dma((ROUNDS,)), dma((ROUNDS,)), dma((ROUNDS,)),
            dma((GROUP,)), dma((GROUP,)), dma((ZS,)), dma((ZS,)), dma((GROUP,)), dma((GROUP,)),
        ],
        compiler_params=pltpu.CompilerParams(
            collective_id=0, has_side_effects=True, vmem_limit_bytes=48 * 1024 * 1024),
        cost_estimate=pl.CostEstimate(flops=4_500_000_000, bytes_accessed=6_000_000, transcendentals=1_000_000),
    )
    args = (features, w_self, w_neigh, cotangent, neighbours.T, send_rows.reshape(ROUNDS, 1, CAP), send_count)
    args = tuple(pltpu.with_memory_space_constraint(one, pltpu.HBM) for one in args)
    return pl.pallas_call(
        hand_over,
        out_shape=tuple(pltpu.HBM(*one) for one in shapes),
        in_specs=[vmem] * 4,
        out_specs=(hbm,) * 4,
        scratch_shapes=[dma((4,))],
    )(*[pltpu.with_memory_space_constraint(one, pltpu.VMEM) for one in call(*args)])


def solution(mesh):
    placed = (
        P("dom", None), P(), P(), P("dom", None), P("dom", None), P("dom", None, None), P("dom", None),
    )
    return jax.shard_map(
        on_device,
        mesh=mesh,
        in_specs=placed,
        out_specs=(P("dom", None), P("dom", None), P(), P()),
        check_vma=False,
    )
```

time: 48.3 us -> 43.1 us (0.89)
  Pallas kernels: 47.4 us -> 42.3 us
    pallas_call x1, Pallas kernels: 46 us -> 40.9 us  [on_device(): call(*args)]
where the time goes in v3:
time: 43.1 us; the launch traced here: 43 us
  Pallas kernels  42.3 us (98%)
  between operations  0.64 us (1%)
    pallas_call x1, Pallas kernels, on_device(): call(*args)  40.9 us
    pallas_call x1, Pallas kernels, on_device(): pl.pallas_call(hand_over, out_shape=tuple((pltpu.HBM(*one) for one in sha...  1.43 us

profile of v3, /device:TPU:1, one launch (start us, length us, event | category | flops | bytes accessed | tf_op | source)
XLA Modules:
  0.0 43.0 jit_solution(14009898520668208228)
XLA Ops:
  0.6 40.9 %shard_map.102 = (bf16[2048,256]{1,0:T(8,128)(2,1)S(1)}, f32[2048,128]{1,0:T(8,128)S(1)}, f32[128,256]{1,0:T(8,128)S(1)}, f32[128,256]{1,0:T(8,128)S(1)}) custom-call(bf16[2048,128]{1,0:T(8,128)(2,1)} %feat_hbm.1, bf16[128,256]{1,0:T(8,128)(2,1)} %ws_hbm.1, bf16[128,256]{1,0:T(8,128)(2,1)} %wn_hbm.1, bf16[2048,256]{1,0:T(8,128)(2,1)} %cot_hbm.1, ...), custom_call_target="tpu_custom_call" | custom-call | flops 4499999744 | bytes 6000000 | tf_op jit(solution)/shard_map/pallas_call | solution.py:357
  41.5 1.4 %shard_map.103 = (bf16[2048,256]{1,0:T(8,128)(2,1)}, f32[2048,128]{1,0:T(8,128)}, f32[128,256]{1,0:T(8,128)}, f32[128,256]{1,0:T(8,128)}) custom-call(bf16[2048,256]{1,0:T(8,128)(2,1)S(1)} %get-tuple-element.8.hid, f32[2048,128]{1,0:T(8,128)S(1)} %get-tuple-element.9.gf, f32[128,256]{1,0:T(8,128)S(1)} %get-tuple-element.10.gws, ...), custom_call_target="tpu_custom_call" | custom-call | tf_op jit(solution)/shard_map/pallas_call | solution.py:351

commit v4 on v3

v4 whole, which is shorter than its diff:
```python
import functools

import jax
import jax.numpy as jnp
from jax import lax
from jax.experimental import pallas as pl
from jax.experimental.pallas import tpu as pltpu
from jax.sharding import PartitionSpec as P

FAN = 10
ROUNDS = 5
CAP = 256
ROWS = 2048
EXT = ROWS + ROUNDS * CAP
D = 128
H = 256
GROUP = 16
ZS = 8
WORDS = 13
DIGITS = 8
SPAN = EXT // DIGITS
MESH = pl.DeviceIdType.MESH
f32, bf16, i32 = jnp.float32, jnp.bfloat16, jnp.int32
ORDER = (3, 2, 1, 4, 0)


def ring(step, size):
    return min(step, size - step)


PLANE = sorted(
    ((dy, dx) for dy in range(4) for dx in range(4)),
    key=lambda t: (t != (0, 0), ring(t[0], 4) + ring(t[1], 4)), reverse=True)
LINE = sorted(range(8), key=lambda t: (t != 0, ring(t, 8)), reverse=True)


def partner_of(me, b):
    bit = lax.rem(lax.div(me, 2**b), 2)
    return me + (1 - 2 * bit) * 2**b


def power(digit):
    return min(digit, 6)


def spans(start, stop):
    cuts = [start] + [d * SPAN for d in range(1, DIGITS) if start < d * SPAN < stop] + [stop]
    return [(lo - start, hi - start, 16.0 ** -power(lo // SPAN)) for lo, hi in zip(cuts[:-1], cuts[1:])]


def lane_scale(start, count):
    row = lax.broadcasted_iota(i32, (1, count), 1)
    out = jnp.zeros((1, count), f32)
    for lo, hi, factor in spans(start, start + count):
        out = jnp.where(row >= lo, factor, out)
    return out.astype(bf16)


def build_counts(l, nbt_ref, val_ref, ct_ref):
    nb = nbt_ref[:, pl.ds(l, 128)]
    digit = (nb * 2521) >> 20
    rest = nb - digit * SPAN
    one = jnp.int32(1) << (4 * digit)
    group = rest >> 5
    val_ref[0] = rest & 31
    for q in range(WORDS):
        val_ref[1 + q] = jnp.where(group == q, one, 0)
    for half in range(2):
        rid = lax.broadcasted_iota(i32, (16, 128), 0) + 16 * half
        acc = [jnp.zeros((16, 128), i32)] * WORDS
        for k in range(FAN):
            hit = val_ref[0, k : k + 1, :] == rid
            for q in range(WORDS):
                acc[q] = acc[q] + jnp.where(hit, val_ref[1 + q, k : k + 1, :], 0)
        for q in range(WORDS):
            for s in range(DIGITS):
                row = s * SPAN + q * 32 + half * 16
                word = acc[q] if s < 7 else lax.shift_right_logical(acc[q], jnp.int32(4))
                count = word & jnp.int32(15 << (4 * power(s)))
                ct_ref[row : row + 16, pl.ds(l, 128)] = count.astype(f32).astype(bf16)


def kernel(
    feat_hbm, ws_hbm, wn_hbm, cot_hbm, nbt_hbm, rows_hbm, live_hbm,
    hidv, own, gws_ref, gwn_ref,
    ws_ref, wn_ref, nbt_ref, rows_ref, live_ref, stl, ct, pt, fv, xt, tt, cotv, gm, hs, hr, bs, br,
    wcat, wt, val, gw, gwc, rsr, zr, pair, agr, rows_s, ff, picked,
    in_sem, hs_s, hs_r, bs_s, bs_r, rs_s, rs_r, z_s, z_r, pair_sem, ag_s, ag_r,
):
    fetch = [
        pltpu.make_async_copy(src, dst, in_sem.at[i])
        for i, (src, dst) in enumerate((
            (rows_hbm, rows_ref), (live_hbm, live_ref), (feat_hbm, fv), (nbt_hbm, nbt_ref),
            (ws_hbm, ws_ref), (wn_hbm, wn_ref), (cot_hbm, cotv), (rows_hbm, rows_s)))
    ]
    for i in (2, 7, 0, 1, 3, 4, 5, 6):
        fetch[i].start()

    me = lax.axis_index("dom")
    core = lax.rem(me, 2)
    z = lax.rem(lax.div(me, 2), ZS)
    x = lax.rem(lax.div(me, 16), 4)
    y = lax.div(me, 64)
    zs = [z] + [lax.rem(z + d, ZS) for d in range(1, ZS)]
    xs = [x] + [lax.rem(x + d, 4) for d in range(1, 4)]
    ys = [y] + [lax.rem(y + d, 4) for d in range(1, 4)]
    spot = y * 4 + x
    twin = me + 1 - 2 * core

    def turned(step, back):
        return ((4 - step[0]) % 4, (4 - step[1]) % 4) if back else step

    def at_plane(step, back=False):
        dy, dx = turned(step, back)
        return ys[dy] * 64 + xs[dx] * 16 + z * 2 + core

    def place(step, back=False):
        dy, dx = turned(step, back)
        return ys[dy] * 4 + xs[dx]

    def line(step, back=False):
        return zs[(ZS - step) % ZS if back else step]

    def at_line(step, back=False):
        return y * 64 + x * 16 + line(step, back) * 2 + core

    barrier = pltpu.get_barrier_semaphore()
    for step in LINE[:-1]:
        pl.semaphore_signal(barrier, inc=1, device_id=(at_line(step),), device_id_type=MESH)
    for step in PLANE[:-1]:
        pl.semaphore_signal(barrier, inc=1, device_id=(at_plane(step),), device_id_type=MESH)

    pl.semaphore_signal(barrier, inc=1, device_id=(twin,), device_id_type=MESH)

    def halo(b):
        return pltpu.make_async_remote_copy(
            src_ref=hs.at[b], dst_ref=hr.at[b], send_sem=hs_s.at[b], recv_sem=hs_r.at[b],
            device_id=(partner_of(me, b),), device_id_type=MESH)

    fetch[2].wait()
    ff[...] = fv[...].astype(f32)
    for i in (0, 1, 7):
        fetch[i].wait()
    for at, b in enumerate(ORDER):
        def load(i, c, b=b):
            r = pl.multiple_of(i * 128, 128)
            for t in range(128):
                picked[pl.ds(r + t, 1), :] = ff[pl.ds(rows_s[2 * b + i, 0, t], 1), :]
            return c

        lax.fori_loop(0, CAP // 128, load, 0)
        live = lax.broadcasted_iota(i32, (CAP, D), 0) < live_ref[0:1, b : b + 1]
        hs[b] = jnp.where(live, picked[...], 0.0).astype(bf16)
        if at == 0:
            pl.semaphore_wait(barrier, GROUP + ZS - 1)
        if b:
            halo(b).start()

    for s in range(4):
        piece = fv[512 * s : 512 * (s + 1), :].T
        xt[0:D, 512 * s : 512 * (s + 1)] = piece
        tt[:, 512 * s : 512 * (s + 1)] = piece * lane_scale(512 * s, 512)

    def owners(b):
        slot = lax.broadcasted_iota(i32, (1, CAP), 1)
        key = jnp.where(slot < live_ref[0:1, b : b + 1], jnp.concatenate([rows_ref[2 * b], rows_ref[2 * b + 1]], axis=1), -1)

        def pick(i, c):
            r = pl.multiple_of(i * 512, 512)
            hit = key == lax.broadcasted_iota(i32, (512, CAP), 0) + r
            pt[pl.ds(r, 512), b * CAP : (b + 1) * CAP] = jnp.where(hit, 1.0, 0.0).astype(bf16)
            return c

        lax.fori_loop(0, ROWS // 512, pick, 0)

    fetch[3].wait()

    def build(i, c):
        build_counts(pl.multiple_of(i * 128, 128), nbt_ref, val, ct)
        return c

    lax.fori_loop(0, ROWS // 128, build, 0)
    halo(0).start()
    stl[...] = jnp.dot(tt[...], ct[0:ROWS, :], preferred_element_type=f32)

    for i in (4, 5, 6):
        fetch[i].wait()
    wcat[0:D, :] = ws_ref[...]
    wcat[D : 2 * D, :] = wn_ref[...]
    wt[:, 0:D] = wn_ref[...].T
    wt[:, D : 2 * D] = ws_ref[...].T

    for b in (4, 1, 0, 2, 3):
        halo(b).wait()
        row = ROWS + b * CAP
        part_t = hr[b].T * lane_scale(row, CAP)
        more = jnp.dot(part_t, ct[row : row + CAP, :], preferred_element_type=f32)
        if b != 3:
            stl[...] += more
        else:
            xt[D : 2 * D, :] = ((stl[...] + more) * (1.0 / FAN)).astype(bf16)
    NB = 512

    def pre_of(i):
        l = i * NB
        both_in = jnp.concatenate([fv[l : l + NB, :], xt[D : 2 * D, l : l + NB].T], axis=1)
        return jnp.dot(both_in, wcat[...], preferred_element_type=f32)

    pre = pre_of(0)
    for i in range(ROWS // NB):
        l = i * NB
        later = pre_of(i + 1) if i + 1 < ROWS // NB else None
        sig = 0.5 + 0.5 * jnp.tanh(0.5 * pre)
        silu = pre * sig
        hidv[l : l + NB, :] = silu.astype(bf16)
        slope = sig + silu * (1.0 - sig)
        grad = (cotv[l : l + NB, :].astype(f32) * slope).astype(bf16)
        both = jnp.dot(grad, wt[...], preferred_element_type=f32)
        gm[l : l + NB, :] = (both[:, 0:D] * (1.0 / FAN)).astype(bf16)
        own[l : l + NB, :] = both[:, D : 2 * D]
        pre = later
        add = jnp.dot(xt[:, l : l + NB], grad, preferred_element_type=f32)
        gw[...] = add if i == 0 else gw[...] + add

    for c in range(GROUP):
        gwc[c] = gw[16 * c : 16 * c + 16, :].astype(bf16)

    def rs(j):
        return pltpu.make_async_remote_copy(
            src_ref=gwc.at[place(PLANE[j])], dst_ref=rsr.at[j], send_sem=rs_s.at[j], recv_sem=rs_r.at[j],
            device_id=(at_plane(PLANE[j]),), device_id_type=MESH)

    for j in range(GROUP - 1):
        rs(j).start()

    def spread(row, count):
        return jnp.dot(ct[row : row + count, :], gm[...], preferred_element_type=f32)

    def back(b):
        return pltpu.make_async_remote_copy(
            src_ref=bs.at[b], dst_ref=br.at[pl.ds(b * CAP, CAP)], send_sem=bs_s.at[b], recv_sem=bs_r.at[b],
            device_id=(partner_of(me, b),), device_id_type=MESH)

    for b in ORDER:
        row = ROWS + b * CAP
        g = spread(row, CAP)
        for lo, hi, factor in spans(row, row + CAP):
            bs[b, lo:hi] = (g[lo:hi] * factor).astype(bf16)
        if b:
            back(b).start()

    def local_back(s):
        g = spread(512 * s, 512)
        for lo, hi, factor in spans(512 * s, 512 * (s + 1)):
            own[512 * s + lo : 512 * s + hi, :] += g[lo:hi] * factor

    local_back(0)
    for b in (0, 1, 2):
        owners(b)
    for j in range(GROUP - 1):
        rs(j).wait()
    back(0).start()
    part = gwc[spot].astype(f32)
    for j in range(GROUP - 1):
        part = part + rsr[j].astype(f32)
    zr[z] = part.astype(bf16)

    def zx(j):
        return pltpu.make_async_remote_copy(
            src_ref=zr.at[z], dst_ref=zr.at[z], send_sem=z_s.at[j], recv_sem=z_r.at[j],
            device_id=(at_line(LINE[j]),), device_id_type=MESH)

    for j in range(ZS - 1):
        zx(j).start()
    for s in (1, 2, 3):
        local_back(s)
    for b in (3, 4):
        owners(b)

    def z_wait(j):
        zx(j).wait_send()
        pltpu.make_async_remote_copy(
            src_ref=zr.at[z], dst_ref=zr.at[line(LINE[j], True)], send_sem=z_s.at[j], recv_sem=z_r.at[j],
            device_id=(at_line(LINE[j], True),), device_id_type=MESH).wait_recv()

    for j in range(ZS - 1):
        z_wait(j)
    full = zr[0].astype(f32)
    for j in range(1, ZS):
        full = full + zr[j].astype(f32)
    pair[0] = full
    swap = pltpu.make_async_remote_copy(
        src_ref=pair.at[0], dst_ref=pair.at[1], send_sem=pair_sem.at[0], recv_sem=pair_sem.at[1],
        device_id=(twin,), device_id_type=MESH)
    swap.start()
    swap.wait()
    agr[spot] = ((pair[0] + pair[1]) * (2.0**-9.5)).astype(bf16)

    def ag(j):
        return pltpu.make_async_remote_copy(
            src_ref=agr.at[spot], dst_ref=agr.at[spot], send_sem=ag_s.at[j], recv_sem=ag_r.at[j],
            device_id=(at_plane(PLANE[j]),), device_id_type=MESH)

    for j in range(GROUP - 1):
        ag(j).start()

    for b in ORDER:
        back(b).wait()

    for i in range(ROWS // NB):
        own[NB * i : NB * (i + 1), :] += jnp.dot(
            pt[NB * i : NB * (i + 1), :], br[...], preferred_element_type=f32)

    def ag_wait(j):
        ag(j).wait_send()
        pltpu.make_async_remote_copy(
            src_ref=agr.at[spot], dst_ref=agr.at[place(PLANE[j], True)], send_sem=ag_s.at[j], recv_sem=ag_r.at[j],
            device_id=(at_plane(PLANE[j], True),), device_id_type=MESH).wait_recv()

    for j in range(GROUP - 1):
        ag_wait(j)
    for c in range(GROUP):
        ref = gws_ref if c < GROUP // 2 else gwn_ref
        r = 16 * (c % (GROUP // 2))
        ref[r : r + 16, :] = agr[c].astype(f32)


def hand_over(hid, gf, gws, gwn, hid_out, gf_out, gws_out, gwn_out, sem):
    copies = [
        pltpu.make_async_copy(src, dst, sem.at[i])
        for i, (src, dst) in enumerate(((hid, hid_out), (gf, gf_out), (gws, gws_out), (gwn, gwn_out)))
    ]
    for one in copies:
        one.start()
    for one in copies:
        one.wait()


def on_device(features, w_self, w_neigh, cotangent, neighbours, send_rows, send_count):
    vmem = pl.BlockSpec(memory_space=pltpu.VMEM)
    hbm = pl.BlockSpec(memory_space=pl.ANY)
    dma = pltpu.SemaphoreType.DMA
    shapes = (((ROWS, H), bf16), ((ROWS, D), f32), ((D, H), f32), ((D, H), f32))
    call = pl.pallas_call(
        kernel,
        out_shape=tuple(pltpu.VMEM(*one) for one in shapes),
        in_specs=[hbm] * 7,
        out_specs=(vmem,) * 4,
        scratch_shapes=[
            pltpu.VMEM((D, H), bf16),
            pltpu.VMEM((D, H), bf16),
            pltpu.VMEM((FAN, ROWS), i32),
            pltpu.VMEM((2 * ROUNDS, 1, CAP // 2), i32),
            pltpu.VMEM((1, ROUNDS), i32),
            pltpu.VMEM((D, ROWS), f32),
            pltpu.VMEM((EXT, ROWS), bf16),
            pltpu.VMEM((ROWS, ROUNDS * CAP), bf16),
            pltpu.VMEM((ROWS, D), bf16),
            pltpu.VMEM((2 * D, ROWS), bf16),
            pltpu.VMEM((D, ROWS), bf16),
            pltpu.VMEM((ROWS, H), bf16),
            pltpu.VMEM((ROWS, D), bf16),
            pltpu.VMEM((ROUNDS, CAP, D), bf16),
            pltpu.VMEM((ROUNDS, CAP, D), bf16),
            pltpu.VMEM((ROUNDS, CAP, D), bf16),
            pltpu.VMEM((ROUNDS * CAP, D), bf16),
            pltpu.VMEM((2 * D, H), bf16),
            pltpu.VMEM((H, 2 * D), bf16),
            pltpu.VMEM((1 + WORDS, FAN, 128), i32),
            pltpu.VMEM((2 * D, H), f32),
            pltpu.VMEM((GROUP, 16, H), bf16),
            pltpu.VMEM((GROUP, 16, H), bf16),
            pltpu.VMEM((ZS, 16, H), bf16),
            pltpu.VMEM((2, 16, H), f32),
            pltpu.VMEM((GROUP, 16, H), bf16),
            pltpu.SMEM((2 * ROUNDS, 1, CAP // 2), i32),
            pltpu.VMEM((ROWS, D), f32),
            pltpu.VMEM((CAP, D), f32),
            dma((8,)),
            dma((ROUNDS,)), dma((ROUNDS,)), dma((ROUNDS,)), dma((ROUNDS,)),
            dma((GROUP,)), dma((GROUP,)), dma((ZS,)), dma((ZS,)), dma((2,)), dma((GROUP,)), dma((GROUP,)),
        ],
        compiler_params=pltpu.CompilerParams(
            collective_id=0, has_side_effects=True, vmem_limit_bytes=48 * 1024 * 1024),
        cost_estimate=pl.CostEstimate(flops=4_500_000_000, bytes_accessed=6_000_000, transcendentals=1_000_000),
    )
    args = (features, w_self, w_neigh, cotangent, neighbours.T, send_rows.reshape(2 * ROUNDS, 1, CAP // 2), send_count)
    args = tuple(pltpu.with_memory_space_constraint(one, pltpu.HBM) for one in args)
    return pl.pallas_call(
        hand_over,
        out_shape=tuple(pltpu.HBM(*one) for one in shapes),
        in_specs=[vmem] * 4,
        out_specs=(hbm,) * 4,
        scratch_shapes=[dma((4,))],
    )(*[pltpu.with_memory_space_constraint(one, pltpu.VMEM) for one in call(*args)])


def solution(mesh):
    placed = (
        P("dom", None), P(), P(), P("dom", None), P("dom", None), P("dom", None, None), P("dom", None),
    )
    return jax.shard_map(
        on_device,
        mesh=mesh,
        in_specs=placed,
        out_specs=(P("dom", None), P("dom", None), P(), P()),
        check_vma=False,
    )
```

time: 43.1 us -> 40.9 us (0.949)
  Pallas kernels: 42.3 us -> 40.1 us
    pallas_call x1, Pallas kernels: 40.9 us -> 38.7 us  [on_device(): call(*args)]
where the time goes in v4:
time: 40.9 us; the launch traced here: 40.8 us
  Pallas kernels  40.1 us (98%)
  between operations  0.64 us (2%)
    pallas_call x1, Pallas kernels, on_device(): call(*args)  38.7 us
    pallas_call x1, Pallas kernels, on_device(): pl.pallas_call(hand_over, out_shape=tuple((pltpu.HBM(*one) for one in sha...  1.43 us

profile of v4, /device:TPU:1, one launch (start us, length us, event | category | flops | bytes accessed | tf_op | source)
XLA Modules:
  0.0 40.8 jit_solution(13817450580315707139)
XLA Ops:
  0.6 38.7 %shard_map.102 = (bf16[2048,256]{1,0:T(8,128)(2,1)S(1)}, f32[2048,128]{1,0:T(8,128)S(1)}, f32[128,256]{1,0:T(8,128)S(1)}, f32[128,256]{1,0:T(8,128)S(1)}) custom-call(bf16[2048,128]{1,0:T(8,128)(2,1)} %feat_hbm.1, bf16[128,256]{1,0:T(8,128)(2,1)} %ws_hbm.1, bf16[128,256]{1,0:T(8,128)(2,1)} %wn_hbm.1, bf16[2048,256]{1,0:T(8,128)(2,1)} %cot_hbm.1, ...), custom_call_target="tpu_custom_call" | custom-call | flops 4499999744 | bytes 6000000 | tf_op jit(solution)/shard_map/pallas_call | solution.py:395
  39.3 1.4 %shard_map.103 = (bf16[2048,256]{1,0:T(8,128)(2,1)}, f32[2048,128]{1,0:T(8,128)}, f32[128,256]{1,0:T(8,128)}, f32[128,256]{1,0:T(8,128)}) custom-call(bf16[2048,256]{1,0:T(8,128)(2,1)S(1)} %get-tuple-element.8.hid, f32[2048,128]{1,0:T(8,128)S(1)} %get-tuple-element.9.gf, f32[128,256]{1,0:T(8,128)S(1)} %get-tuple-element.10.gws, ...), custom_call_target="tpu_custom_call" | custom-call | tf_op jit(solution)/shard_map/pallas_call | solution.py:389

commit v5 on v4

--- a/solution.py
+++ b/solution.py
@@ -141,7 +141,7 @@
     ff[...] = fv[...].astype(f32)
     for i in (0, 1, 7):
         fetch[i].wait()
-    for at, b in enumerate(ORDER):
+    for b in ORDER:
         def load(i, c, b=b):
             r = pl.multiple_of(i * 128, 128)
             for t in range(128):
@@ -151,10 +151,6 @@
         lax.fori_loop(0, CAP // 128, load, 0)
         live = lax.broadcasted_iota(i32, (CAP, D), 0) < live_ref[0:1, b : b + 1]
         hs[b] = jnp.where(live, picked[...], 0.0).astype(bf16)
-        if at == 0:
-            pl.semaphore_wait(barrier, GROUP + ZS - 1)
-        if b:
-            halo(b).start()
 
     for s in range(4):
         piece = fv[512 * s : 512 * (s + 1), :].T
@@ -173,6 +169,11 @@
 
         lax.fori_loop(0, ROWS // 512, pick, 0)
 
+    for b in (0, 1):
+        owners(b)
+    pl.semaphore_wait(barrier, GROUP + ZS - 1)
+    for b in ORDER[:-1]:
+        halo(b).start()
     fetch[3].wait()
 
     def build(i, c):
@@ -255,7 +256,7 @@
             own[512 * s + lo : 512 * s + hi, :] += g[lo:hi] * factor
 
     local_back(0)
-    for b in (0, 1, 2):
+    for b in (2,):
         owners(b)
     for j in range(GROUP - 1):
         rs(j).wait()

time: 40.9 us -> 40.7 us (level)
  no operation moved by 1% of the time
where the time goes in v5:
time: 40.7 us; the launch traced here: 40.6 us
  Pallas kernels  39.9 us (98%)
  between operations  0.64 us (2%)
    pallas_call x1, Pallas kernels, on_device(): call(*args)  38.5 us
    pallas_call x1, Pallas kernels, on_device(): pl.pallas_call(hand_over, out_shape=tuple((pltpu.HBM(*one) for one in sha...  1.43 us

profile of v5, /device:TPU:1, one launch (start us, length us, event | category | flops | bytes accessed | tf_op | source)
XLA Modules:
  0.0 40.6 jit_solution(9842239703624808079)
XLA Ops:
  0.6 38.5 %shard_map.102 = (bf16[2048,256]{1,0:T(8,128)(2,1)S(1)}, f32[2048,128]{1,0:T(8,128)S(1)}, f32[128,256]{1,0:T(8,128)S(1)}, f32[128,256]{1,0:T(8,128)S(1)}) custom-call(bf16[2048,128]{1,0:T(8,128)(2,1)} %feat_hbm.1, bf16[128,256]{1,0:T(8,128)(2,1)} %ws_hbm.1, bf16[128,256]{1,0:T(8,128)(2,1)} %wn_hbm.1, bf16[2048,256]{1,0:T(8,128)(2,1)} %cot_hbm.1, ...), custom_call_target="tpu_custom_call" | custom-call | flops 4499999744 | bytes 6000000 | tf_op jit(solution)/shard_map/pallas_call | solution.py:396
  39.2 1.4 %shard_map.103 = (bf16[2048,256]{1,0:T(8,128)(2,1)}, f32[2048,128]{1,0:T(8,128)}, f32[128,256]{1,0:T(8,128)}, f32[128,256]{1,0:T(8,128)}) custom-call(bf16[2048,256]{1,0:T(8,128)(2,1)S(1)} %get-tuple-element.8.hid, f32[2048,128]{1,0:T(8,128)S(1)} %get-tuple-element.9.gf, f32[128,256]{1,0:T(8,128)S(1)} %get-tuple-element.10.gws, ...), custom_call_target="tpu_custom_call" | custom-call | tf_op jit(solution)/shard_map/pallas_call | solution.py:390

commit v6 on v5

--- a/solution.py
+++ b/solution.py
@@ -273,7 +273,7 @@
 
     for j in range(ZS - 1):
         zx(j).start()
-    for s in (1, 2, 3):
+    for s in (1, 2):
         local_back(s)
     for b in (3, 4):
         owners(b)
@@ -294,6 +294,7 @@
         src_ref=pair.at[0], dst_ref=pair.at[1], send_sem=pair_sem.at[0], recv_sem=pair_sem.at[1],
         device_id=(twin,), device_id_type=MESH)
     swap.start()
+    local_back(3)
     swap.wait()
     agr[spot] = ((pair[0] + pair[1]) * (2.0**-9.5)).astype(bf16)
 

time: 40.7 us -> 40.6 us (level)
  no operation moved by 1% of the time
where the time goes in v6:
time: 40.6 us; the launch traced here: 40.5 us
  Pallas kernels  39.8 us (98%)
  between operations  0.64 us (2%)
    pallas_call x1, Pallas kernels, on_device(): call(*args)  38.4 us
    pallas_call x1, Pallas kernels, on_device(): pl.pallas_call(hand_over, out_shape=tuple((pltpu.HBM(*one) for one in sha...  1.43 us

profile of v6, /device:TPU:1, one launch (start us, length us, event | category | flops | bytes accessed | tf_op | source)
XLA Modules:
  0.0 40.5 jit_solution(5001194114758880043)
XLA Ops:
  0.6 38.4 %shard_map.102 = (bf16[2048,256]{1,0:T(8,128)(2,1)S(1)}, f32[2048,128]{1,0:T(8,128)S(1)}, f32[128,256]{1,0:T(8,128)S(1)}, f32[128,256]{1,0:T(8,128)S(1)}) custom-call(bf16[2048,128]{1,0:T(8,128)(2,1)} %feat_hbm.1, bf16[128,256]{1,0:T(8,128)(2,1)} %ws_hbm.1, bf16[128,256]{1,0:T(8,128)(2,1)} %wn_hbm.1, bf16[2048,256]{1,0:T(8,128)(2,1)} %cot_hbm.1, ...), custom_call_target="tpu_custom_call" | custom-call | flops 4499999744 | bytes 6000000 | tf_op jit(solution)/shard_map/pallas_call | solution.py:397
  39.1 1.4 %shard_map.103 = (bf16[2048,256]{1,0:T(8,128)(2,1)}, f32[2048,128]{1,0:T(8,128)}, f32[128,256]{1,0:T(8,128)}, f32[128,256]{1,0:T(8,128)}) custom-call(bf16[2048,256]{1,0:T(8,128)(2,1)S(1)} %get-tuple-element.8.hid, f32[2048,128]{1,0:T(8,128)S(1)} %get-tuple-element.9.gf, f32[128,256]{1,0:T(8,128)S(1)} %get-tuple-element.10.gws, ...), custom_call_target="tpu_custom_call" | custom-call | tf_op jit(solution)/shard_map/pallas_call | solution.py:391
